TPU v7x, 32 devices: a whole 2x2x4 slice. The times are simulated.
32 devices in a mesh: rows: 8 (over z, y), feat: 4 (over x, core).
Axes of the slice: x: 2, y: 2, z: 4, core: 2. Of those that a mesh axis runs over, the one named last changes fastest.
Arguments:
- gradient: float32 [131072], P('rows'), may hold values from -6 to 6
- hessian: bfloat16 [131072], P('rows'), may hold values from 0.049804688 to 1
- groups: int32 [131072], P('rows'), may hold values from 0 to 4095
- leaf_ids: int32 [131072], P('rows'), may hold values from 0 to 31
- bins: int32 [256, 131072], P('feat', 'rows'), may hold values from 0 to 63
- group_sizes: int32 [4096], P('rows'), may hold values from 16 to 63
- variance_ratio: float32 [1], replicated, may hold values from 1 to 16
Outputs:
- histograms: float32 [32, 256, 128], P('rows', 'feat')
- group_means: float32 [4096], P('rows')
All inputs are finite; a program needn't handle non-finite values.
Results may differ from a plain program's by a relative error of at most 0.00038.
Values sent between devices are 32-bit elements; how exact they have to be, the bound alone decides.
No kernel may reach another device: no remote copies, remote signals or barrier semaphores. Data moves between devices by JAX's collectives and lax.ppermute only.
A program may use at most 64 MiB of HBM per device.

v0:
```python
import jax
import jax.numpy as jnp
from jax import lax
from jax.sharding import PartitionSpec as P

BINS = 64
LEAVES = 32


def hist_term(leaf_ids, weights, bin_rows, leaf_count, bins_n):
    channels = len(weights)
    feature_count, row_count = bin_rows.shape
    block_rows = min(2048, row_count)
    turn_count = row_count // block_rows
    levels = jnp.arange(bins_n, dtype=jnp.int32)
    wanted = jnp.arange(leaf_count, dtype=jnp.int32)
    stacked = jnp.stack(weights)

    def advance(turn_no, summed):
        offset = turn_no * block_rows
        leaf_block = lax.dynamic_slice_in_dim(leaf_ids, offset, block_rows, 0)
        weight_block = lax.dynamic_slice_in_dim(stacked, offset, block_rows, 1)
        bin_block = lax.dynamic_slice_in_dim(bin_rows, offset, block_rows, 1)
        member = (leaf_block[None, :] == wanted[:, None]).astype(jnp.bfloat16)
        left_side = (member[:, None, :] * weight_block[None, :, :]).reshape(
            leaf_count * channels, block_rows
        )
        right_side = (bin_block[:, None, :] == levels[None, :, None]).astype(jnp.bfloat16)
        right_side = right_side.reshape(feature_count * bins_n, block_rows)
        return summed + lax.dot_general(
            left_side, right_side, (((1,), (1,)), ((), ())), preferred_element_type=jnp.float32
        )

    initial = jnp.zeros((leaf_count * channels, feature_count * bins_n), jnp.float32)
    summed = lax.fori_loop(0, turn_count, advance, initial)
    summed = summed.reshape(leaf_count, channels, feature_count, bins_n).transpose(0, 2, 1, 3)
    return summed.reshape(leaf_count, feature_count, channels * bins_n)


def group_sum_dense(values, ids, group_count):
    high_count = group_count // 128
    row_count = values.shape[0]
    block_rows = min(2048, row_count)
    turn_count = row_count // block_rows
    high_levels = jnp.arange(high_count, dtype=jnp.int32)
    low_levels = jnp.arange(128, dtype=jnp.int32)

    def advance(turn_no, summed):
        offset = turn_no * block_rows
        id_block = lax.dynamic_slice_in_dim(ids, offset, block_rows, 0)
        value_block = lax.dynamic_slice_in_dim(values, offset, block_rows, 0)
        high_hot = (id_block[:, None] // 128 == high_levels[None, :]).astype(jnp.float32)
        low_hot = (id_block[:, None] % 128 == low_levels[None, :]).astype(
            jnp.float32
        ) * value_block[:, None]
        return summed + lax.dot_general(
            high_hot,
            low_hot,
            (((0,), (0,)), ((), ())),
            precision=lax.Precision.HIGHEST,
            preferred_element_type=jnp.float32,
        )

    initial = jnp.zeros((high_count, 128), jnp.float32)
    return lax.fori_loop(0, turn_count, advance, initial).reshape(group_count)


def group_lookup(table, ids):
    high_count = table.shape[0] // 128
    grid = table.reshape(high_count, 128)
    row_count = ids.shape[0]
    block_rows = min(2048, row_count)
    turn_count = row_count // block_rows
    high_levels = jnp.arange(high_count, dtype=jnp.int32)
    low_levels = jnp.arange(128, dtype=jnp.int32)

    def advance(turn_no, result):
        offset = turn_no * block_rows
        id_block = lax.dynamic_slice_in_dim(ids, offset, block_rows, 0)
        high_hot = (id_block[:, None] // 128 == high_levels[None, :]).astype(jnp.float32)
        picked = jnp.dot(
            high_hot, grid, precision=lax.Precision.HIGHEST, preferred_element_type=jnp.float32
        )
        low_hot = id_block[:, None] % 128 == low_levels[None, :]
        found = jnp.sum(jnp.where(low_hot, picked, 0.0), axis=1)
        return lax.dynamic_update_slice_in_dim(result, found, offset, 0)

    initial = jnp.zeros((row_count,), jnp.float32)
    return lax.fori_loop(0, turn_count, advance, initial)


def shards(gradient, hessian, groups, leaf_ids, bins, group_sizes, variance_ratio):
    owners = lax.axis_size("rows")
    own_groups = group_sizes.shape[0]
    group_count = own_groups * owners
    leaf_share = LEAVES // owners
    ratio = variance_ratio[0]
    sharers = lax.axis_size("feat")
    mine = lax.axis_index("feat")
    part_rows = gradient.shape[0] // sharers
    grad_part = lax.dynamic_slice_in_dim(gradient, mine * part_rows, part_rows, 0)
    group_part = lax.dynamic_slice_in_dim(groups, mine * part_rows, part_rows, 0)
    partial_value = group_sum_dense(grad_part, group_part, group_count)
    shares = lax.psum_scatter(partial_value, ("rows", "feat"), scatter_dimension=0, tiled=True)
    share_len = own_groups // sharers
    size_share = lax.dynamic_slice_in_dim(group_sizes, mine * share_len, share_len, 0)
    mean_share = -shares / (size_share.astype(jnp.float32) + ratio)
    all_means = lax.all_gather(mean_share, ("rows", "feat"), axis=0, tiled=True)
    own_means = lax.dynamic_slice_in_dim(
        all_means, lax.axis_index("rows") * own_groups, own_groups, 0
    )
    row_means = group_lookup(all_means, groups)
    adjusted = (gradient + hessian.astype(jnp.float32) * row_means).astype(jnp.bfloat16)
    histograms = lax.psum_scatter(
        hist_term(leaf_ids, (adjusted, hessian), bins, leaf_share * lax.axis_size("rows"), BINS),
        "rows",
        scatter_dimension=0,
        tiled=True,
    )
    return (histograms, own_means)


def solution(mesh):
    in_specs = (P("rows"), P("rows"), P("rows"), P("rows"), P("feat", "rows"), P("rows"), P())
    out_specs = (P("rows", "feat", None), P("rows"))
    return jax.shard_map(shards, mesh=mesh, in_specs=in_specs, out_specs=out_specs, check_vma=False)
```

profile of v0, /device:TPU:0, one launch (start us, length us, event | category | flops | bytes accessed | tf_op | source)
XLA Modules:
  0.0 352.6 jit_solution(7495840666002521499)
XLA Ops:
  9.4 3.9 %while.47 = (s32[]{:T(128)}, f32[32,128]{1,0:T(8,128)S(1)}, s32[4096]{0:T(1024)S(1)}, f32[4096]{0:T(1024)S(1)}, s32[]{:T(128)}, /*index=5*/s32[]{:T(128)}, s32[]{:T(128)}, s32[]{:T(128)}) while((s32[]{:T(128)}, f32[32,128]{1,0:T(8,128)S(1)}, s32[4096]{0:T(1024)S(1)}, f32[4096]{0:T(1024)S(1)}, s32[]{:T(128)}, /*index=5*/s32[]{:T(128)}, ...), condition=%wide.region_1.2_spmd.clone, body=%wide.region_0.1_spmd.clone.sunk | while | flops 101312520 | bytes 110753 | solution.py:65
  13.2 42.1 %all-reduce = f32[4096]{0:T(1024)S(1)} all-reduce(f32[4096]{0:T(1024)S(1)} %bitcast.26), channel_id=2, replica_groups=mesh['rows'=8,'feat'=4] {'rows','feat'}, use_global_device_ids=true, to_apply=%region_2.3.clone | all-reduce | flops 4096 | bytes 32768
  56.1 40.0 %all-gather = f32[32,1,128]{2,1,0:T(1,128)S(1)} all-gather(f32[1,1,128]{2,1,0:T(1,128)S(1)} %fusion.24), channel_id=1, replica_groups=mesh['rows'=8,'feat'=4] {'rows','feat'}, dimensions={0}, use_global_device_ids=true | all-gather | bytes 16896 | tf_op jit(solution)/shard_map/all_gather | solution.py:108
  96.9 23.4 %while.46 = (s32[]{:T(128)}, f32[16384]{0:T(1024)S(1)}, s32[16384]{0:T(1024)}, f32[32,128]{1,0:T(8,128)S(1)}, s32[]{:T(128)}, /*index=5*/s32[]{:T(128)}, s32[]{:T(128)}, s32[]{:T(128)}) while((s32[]{:T(128)}, f32[16384]{0:T(1024)S(1)}, s32[16384]{0:T(1024)}, f32[32,128]{1,0:T(8,128)S(1)}, s32[]{:T(128)}, /*index=5*/s32[]{:T(128)}, ...), condition=%wide.region_5.6_spmd.clone, body=%wide.region_3.5_spmd.clone.sunk | while | flops 101564424 | bytes 94351 | solution.py:89
  120.5 158.3 %while.48 = (s32[]{:T(128)}, f32[64,4096]{1,0:T(8,128)S(1)}, s32[16384]{0:T(1024)}, bf16[2,16384]{1,0:T(2,128)(2,1)S(1)}, s32[64,16384]{1,0:T(8,128)}, /*index=5*/s32[]{:T(128)}, s32[]{:T(128)}, s32[]{:T(128)}, s32[]{:T(128)}) while((s32[]{:T(128)}, f32[64,4096]{1,0:T(8,128)S(1)}, s32[16384]{0:T(1024)}, ...), condition=%wide.region_7.8_spmd.clone, body=%wide.region_6.7_spmd.clone.sunk | while | flops 1082916864 | bytes 21807272 | solution.py:35
  122.8 8.9 %iota_compare_fusion.14 = pred[64,64,2048]{2,1,0:T(32,128)(4,1)} fusion(s32[64,2048]{1,0:T(8,128)S(1)} %constant_dynamic-slice_fusion.5), kind=kLoop, calls=%fused_computation.38.clone.1 | loop fusion | flops 8388608 | bytes 8912896 | tf_op jit(solution)/shard_map/while/body/eval_jaxpr/eq | solution.py:28
  131.6 8.6 %convolution_add_fusion.5 = f32[64,4096]{1,0:T(8,128)S(1)} fusion(bf16[64,2048]{1,0:T(8,128)(2,1)S(1)} %mul.142, pred[4096,2048]{1,0:T(32,128)(4,1)} %bitcast.22, f32[64,4096]{1,0:T(8,128)S(1)} %get-tuple-element.672, pred[]{:T(512)S(6)} %compare.33), kind=kOutput, calls=%fused_computation.39.clone.1 | convolution fusion | flops 1074266112 | bytes 10747905 | tf_op jit(solution)/shard_map/while/body/eval_jaxpr/dot_general | solution.py:30
  142.5 8.9 %iota_compare_fusion.14 = pred[64,64,2048]{2,1,0:T(32,128)(4,1)} fusion(s32[64,2048]{1,0:T(8,128)S(1)} %constant_dynamic-slice_fusion.5), kind=kLoop, calls=%fused_computation.38.clone.1 | loop fusion | flops 8388608 | bytes 8912896 | tf_op jit(solution)/shard_map/while/body/eval_jaxpr/eq | solution.py:28
  151.4 8.6 %convolution_add_fusion.5 = f32[64,4096]{1,0:T(8,128)S(1)} fusion(bf16[64,2048]{1,0:T(8,128)(2,1)S(1)} %mul.142, pred[4096,2048]{1,0:T(32,128)(4,1)} %bitcast.22, f32[64,4096]{1,0:T(8,128)S(1)} %get-tuple-element.672, pred[]{:T(512)S(6)} %compare.33), kind=kOutput, calls=%fused_computation.39.clone.1 | convolution fusion | flops 1074266112 | bytes 10747905 | tf_op jit(solution)/shard_map/while/body/eval_jaxpr/dot_general | solution.py:30
  162.3 8.9 %iota_compare_fusion.14 = pred[64,64,2048]{2,1,0:T(32,128)(4,1)} fusion(s32[64,2048]{1,0:T(8,128)S(1)} %constant_dynamic-slice_fusion.5), kind=kLoop, calls=%fused_computation.38.clone.1 | loop fusion | flops 8388608 | bytes 8912896 | tf_op jit(solution)/shard_map/while/body/eval_jaxpr/eq | solution.py:28
  171.2 8.6 %convolution_add_fusion.5 = f32[64,4096]{1,0:T(8,128)S(1)} fusion(bf16[64,2048]{1,0:T(8,128)(2,1)S(1)} %mul.142, pred[4096,2048]{1,0:T(32,128)(4,1)} %bitcast.22, f32[64,4096]{1,0:T(8,128)S(1)} %get-tuple-element.672, pred[]{:T(512)S(6)} %compare.33), kind=kOutput, calls=%fused_computation.39.clone.1 | convolution fusion | flops 1074266112 | bytes 10747905 | tf_op jit(solution)/shard_map/while/body/eval_jaxpr/dot_general | solution.py:30
  182.1 8.9 %iota_compare_fusion.14 = pred[64,64,2048]{2,1,0:T(32,128)(4,1)} fusion(s32[64,2048]{1,0:T(8,128)S(1)} %constant_dynamic-slice_fusion.5), kind=kLoop, calls=%fused_computation.38.clone.1 | loop fusion | flops 8388608 | bytes 8912896 | tf_op jit(solution)/shard_map/while/body/eval_jaxpr/eq | solution.py:28
  190.9 8.6 %convolution_add_fusion.5 = f32[64,4096]{1,0:T(8,128)S(1)} fusion(bf16[64,2048]{1,0:T(8,128)(2,1)S(1)} %mul.142, pred[4096,2048]{1,0:T(32,128)(4,1)} %bitcast.22, f32[64,4096]{1,0:T(8,128)S(1)} %get-tuple-element.672, pred[]{:T(512)S(6)} %compare.33), kind=kOutput, calls=%fused_computation.39.clone.1 | convolution fusion | flops 1074266112 | bytes 10747905 | tf_op jit(solution)/shard_map/while/body/eval_jaxpr/dot_general | solution.py:30
  201.8 8.9 %iota_compare_fusion.14 = pred[64,64,2048]{2,1,0:T(32,128)(4,1)} fusion(s32[64,2048]{1,0:T(8,128)S(1)} %constant_dynamic-slice_fusion.5), kind=kLoop, calls=%fused_computation.38.clone.1 | loop fusion | flops 8388608 | bytes 8912896 | tf_op jit(solution)/shard_map/while/body/eval_jaxpr/eq | solution.py:28
  210.7 8.6 %convolution_add_fusion.5 = f32[64,4096]{1,0:T(8,128)S(1)} fusion(bf16[64,2048]{1,0:T(8,128)(2,1)S(1)} %mul.142, pred[4096,2048]{1,0:T(32,128)(4,1)} %bitcast.22, f32[64,4096]{1,0:T(8,128)S(1)} %get-tuple-element.672, pred[]{:T(512)S(6)} %compare.33), kind=kOutput, calls=%fused_computation.39.clone.1 | convolution fusion | flops 1074266112 | bytes 10747905 | tf_op jit(solution)/shard_map/while/body/eval_jaxpr/dot_general | solution.py:30
  221.6 8.9 %iota_compare_fusion.14 = pred[64,64,2048]{2,1,0:T(32,128)(4,1)} fusion(s32[64,2048]{1,0:T(8,128)S(1)} %constant_dynamic-slice_fusion.5), kind=kLoop, calls=%fused_computation.38.clone.1 | loop fusion | flops 8388608 | bytes 8912896 | tf_op jit(solution)/shard_map/while/body/eval_jaxpr/eq | solution.py:28
  230.4 8.6 %convolution_add_fusion.5 = f32[64,4096]{1,0:T(8,128)S(1)} fusion(bf16[64,2048]{1,0:T(8,128)(2,1)S(1)} %mul.142, pred[4096,2048]{1,0:T(32,128)(4,1)} %bitcast.22, f32[64,4096]{1,0:T(8,128)S(1)} %get-tuple-element.672, pred[]{:T(512)S(6)} %compare.33), kind=kOutput, calls=%fused_computation.39.clone.1 | convolution fusion | flops 1074266112 | bytes 10747905 | tf_op jit(solution)/shard_map/while/body/eval_jaxpr/dot_general | solution.py:30
  241.3 8.9 %iota_compare_fusion.14 = pred[64,64,2048]{2,1,0:T(32,128)(4,1)} fusion(s32[64,2048]{1,0:T(8,128)S(1)} %constant_dynamic-slice_fusion.5), kind=kLoop, calls=%fused_computation.38.clone.1 | loop fusion | flops 8388608 | bytes 8912896 | tf_op jit(solution)/shard_map/while/body/eval_jaxpr/eq | solution.py:28
  250.2 8.6 %convolution_add_fusion.5 = f32[64,4096]{1,0:T(8,128)S(1)} fusion(bf16[64,2048]{1,0:T(8,128)(2,1)S(1)} %mul.142, pred[4096,2048]{1,0:T(32,128)(4,1)} %bitcast.22, f32[64,4096]{1,0:T(8,128)S(1)} %get-tuple-element.672, pred[]{:T(512)S(6)} %compare.33), kind=kOutput, calls=%fused_computation.39.clone.1 | convolution fusion | flops 1074266112 | bytes 10747905 | tf_op jit(solution)/shard_map/while/body/eval_jaxpr/dot_general | solution.py:30
  261.1 8.9 %iota_compare_fusion.14 = pred[64,64,2048]{2,1,0:T(32,128)(4,1)} fusion(s32[64,2048]{1,0:T(8,128)S(1)} %constant_dynamic-slice_fusion.5), kind=kLoop, calls=%fused_computation.38.clone.1 | loop fusion | flops 8388608 | bytes 8912896 | tf_op jit(solution)/shard_map/while/body/eval_jaxpr/eq | solution.py:28
  269.9 8.6 %convolution_add_fusion.5 = f32[64,4096]{1,0:T(8,128)S(1)} fusion(bf16[64,2048]{1,0:T(8,128)(2,1)S(1)} %mul.142, pred[4096,2048]{1,0:T(32,128)(4,1)} %bitcast.22, f32[64,4096]{1,0:T(8,128)S(1)} %get-tuple-element.672, pred[]{:T(512)S(6)} %compare.33), kind=kOutput, calls=%fused_computation.39.clone.1 | convolution fusion | flops 1074266112 | bytes 10747905 | tf_op jit(solution)/shard_map/while/body/eval_jaxpr/dot_general | solution.py:30
  279.6 3.0 copy.12
  282.6 3.3 reshape.157
  286.7 59.1 %reduce-scatter.2.cloned.1.call-done = f32[4,64,128]{2,1,0:T(8,128)} async-done(((f32[32,64,128]{2,1,0:T(8,128)}), f32[4,64,128]{2,1,0:T(8,128)}) %reduce-scatter.2.cloned.1.call-update) | async-done | bytes 131088 | tf_op jit(solution)/shard_map/reduce_scatter | solution.py:114
  (106 shorter events, 49.3 us)
Async XLA Ops:
  7.2 113.1 %copy-start.1 = (f32[16384]{0:T(1024)S(1)}, f32[16384]{0:T(1024)}, u32[]{:S(2)}) copy-start(f32[16384]{0:T(1024)} %param.13) | copy-start | bytes 196612
  7.2 113.1 %copy-start = (bf16[16384]{0:T(1024)(128)(2,1)S(1)}, bf16[16384]{0:T(1024)(128)(2,1)}, u32[]{:S(2)}) copy-start(bf16[16384]{0:T(1024)(128)(2,1)} %param.14) | copy-start | bytes 98308
  7.2 338.5 %reduce-scatter.2.cloned.1.call-start = ((), (), s32[]{:S(2)}) async-start(), calls=%async_computation.1 | async-start | bytes 1179648 | tf_op jit(solution)/shard_map/reduce_scatter | solution.py:114
Sparse Core Ops, SparseCore 0:
  286.1 59.5 reduce-scatter.1
where the time goes:
time: 355 us; the launch traced here: 353 us
  other arithmetic  85.6 us (24%)
  blocking collectives  82.1 us (23%)
  matrix products  82 us (23%)
  waiting for transfers between devices  59.1 us (17%)
  local copies, waits for them, and re-layouts  27.9 us (8%)
  between operations  14.8 us (4%)
    eq x8, other arithmetic, advance(): bin_block[:, None, :] == levels[None, :, None]  70.8 us
    dot_general x8, matrix products, advance(): lax.dot_general(left_side, right_side, (((1,), (1,)), ((), ())), preferre...  69.1 us
    reduce_scatter x1, waiting for transfers between devices, shards(): lax.psum_scatter(hist_term(leaf_ids, (adjusted, hessian), bins, leaf_shar...  59.1 us
    unnamed x1, blocking collectives  42.1 us
    all_gather x1, blocking collectives, shards(): all_means = lax.all_gather(mean_share, ('rows', 'feat'), axis=0, tiled=True)  40 us
    dot_general x8, matrix products, advance(): jnp.dot(high_hot, grid, precision=lax.Precision.HIGHEST, preferred_elemen...  9.19 us
    dynamic_slice x8, local copies, waits for them, and re-layouts, advance(): bin_block = lax.dynamic_slice_in_dim(bin_rows, offset, block_rows, 1)  8.67 us
  transfers between devices with their start and end apart: 1, of which 1 were waited for; matrix products, arithmetic and copies ran while one was open for 0% of the time, Pallas kernels for 0%

commit v1 on v0

v1 whole, which is shorter than its diff:
```python
import functools

import jax
import jax.numpy as jnp
from jax import lax
from jax.experimental import pallas as pl
from jax.experimental.pallas import tpu as pltpu
from jax.sharding import PartitionSpec as P

BINS = 64
LEAVES = 32
LANES = 128
F8 = jnp.float8_e4m3fn
PARAMS = pltpu.CompilerParams(vmem_limit_bytes=48 * 2**20)


def group_sum_kernel(gradient, groups, sizes, message):
    blocks = gradient.shape[0]
    high_count = message.shape[0] // 2
    own = sizes.shape[0]
    me = lax.axis_index("rows")
    exact = gradient[...]
    first = exact.astype(jnp.bfloat16).astype(jnp.float32)
    rest = exact - first
    second = rest.astype(jnp.bfloat16).astype(jnp.float32)
    third = rest - second
    ids = groups[...]
    high, low = lax.shift_right_logical(ids, 7), ids & (LANES - 1)
    high_levels = lax.broadcasted_iota(jnp.int32, (high_count, LANES), 0)
    low_levels = lax.broadcasted_iota(jnp.int32, (LANES, LANES), 0)
    total = jnp.zeros((3 * high_count, LANES), jnp.float32)
    step = min(32, blocks)
    for start in range(0, blocks, step):
        left, right = [], []
        for j in range(start, start + step):
            here = high[j : j + 1] == high_levels
            left.append(
                jnp.concatenate(
                    [jnp.where(here, part[j : j + 1], 0.0) for part in (first, second, third)], 0
                ).astype(jnp.bfloat16)
            )
            right.append(jnp.where(low[j : j + 1] == low_levels, 1.0, 0.0).astype(jnp.bfloat16))
        total += lax.dot_general(
            jnp.concatenate(left, 1),
            jnp.concatenate(right, 1),
            (((1,), (1,)), ((), ())),
            preferred_element_type=jnp.float32,
        )
    message[:high_count] = (
        total[:high_count] + (total[high_count : 2 * high_count] + total[2 * high_count :])
    )
    own_sizes = sizes[...].astype(jnp.float32)
    for owner in range(high_count // own):
        begin = high_count + owner * own
        message[begin : begin + own] = jnp.where(me == owner, own_sizes, 0.0)


def turn_kernel(bins, turned):
    features, rows = bins.shape
    copies = LANES // features
    levels = BINS // copies
    for start in range(0, rows, LANES):
        block = bins[:, start : start + LANES]
        stack = jnp.concatenate([block - p * levels for p in range(copies)], 0)
        turned[start : start + LANES] = stack.T.astype(jnp.int8)


def weigh_kernel(owner_order, message, ratio, gradient, hessian, groups, leaf_ids, left, unscale):
    blocks = gradient.shape[0]
    high_count = message.shape[0] // 2
    me = lax.axis_index("rows")
    owners = len(owner_order)
    share = LEAVES // owners
    means = -message[:high_count] / (message[high_count:] + ratio[0])
    ids = groups[...]
    high, low = lax.shift_right_logical(ids, 7), ids & (LANES - 1)
    found = []
    for j in range(0, blocks, 8):
        low_here, high_here = low[j : j + 8], high[j : j + 8]
        value = jnp.zeros((8, LANES), jnp.float32)
        for h in range(high_count):
            row = jnp.broadcast_to(means[h : h + 1], (8, LANES))
            picked = jnp.take_along_axis(row, low_here, axis=1, mode="promise_in_bounds")
            value = jnp.where(high_here == h, picked, value)
        found.append(value)
    row_means = jnp.concatenate(found, 0)
    curve = hessian[...].astype(jnp.float32)
    adjusted = (gradient[...] + curve * row_means).astype(jnp.bfloat16).astype(jnp.float32)

    level = jnp.max(jnp.abs(adjusted)) * 32.0
    scale, back = jnp.float32(32.0), jnp.float32(1.0 / 32.0)
    for power in (16, 8, 4, 2, 1):
        big = level > 256.0 * 2.0 ** (power - 1)
        level = jnp.where(big, level * 2.0**-power, level)
        scale = jnp.where(big, scale * 2.0**-power, scale)
        back = jnp.where(big, back * 2.0**power, back)
    unscale[...] = jnp.full(unscale.shape, back, jnp.float32)

    scaled = adjusted * scale
    adjusted_high = scaled.astype(F8).astype(jnp.float32)
    adjusted_low = (scaled - adjusted_high) * 16.0
    curve_high = curve.astype(F8).astype(jnp.float32)
    curve_low = (curve - curve_high) * 16.0

    half = 2 * LEAVES
    row = lax.broadcasted_iota(jnp.int32, (half, LANES), 0)
    place = row // (2 * share)
    owner = jnp.zeros_like(place)
    for position, other in enumerate(owner_order):
        owner = jnp.where(place == position, other, owner)
    leaf_of = (owner ^ me) * share + (row % (2 * share)) // 2
    is_gradient = row % 2 == 0
    leaves = leaf_ids[...]
    for j in range(blocks):
        member = leaves[j : j + 1] == leaf_of
        parts = []
        for one, two in ((adjusted_high, curve_high), (adjusted_low, curve_low)):
            both = jnp.where(is_gradient, one[j : j + 1], two[j : j + 1])
            parts.append(jnp.where(member, both, 0.0))
        left[:, j * LANES : (j + 1) * LANES] = jnp.concatenate(parts, 0).astype(F8)


def histogram_kernel(first_level, level_step, turned, left, unscale, keep, send):
    base = first_level + pl.program_id(0) * level_step
    bins = turned[...]
    hot = []
    for q in range(level_step):
        level = (base + q).astype(jnp.int8)
        hot.append(jnp.where(bins == level, jnp.ones((), F8), jnp.zeros((), F8)))
    both = jnp.dot(left[...], jnp.concatenate(hot, 1), preferred_element_type=jnp.float32)
    half = both.shape[0] // 2
    total = both[:half] + both[half:] * 0.0625
    is_gradient = lax.broadcasted_iota(jnp.int32, (half, 1), 0) % 2 == 0
    total = total * jnp.where(is_gradient, unscale[0:1, 0:1], 1.0)
    keep[...] = total[: half // 2]
    send[...] = total[half // 2 :]


def arrange_kernel(own, histograms):
    share, features, _ = histograms.shape
    copies = LANES // features
    levels = BINS // copies
    for l in range(share):
        rows = []
        for channel in range(2):
            r = 2 * l + channel
            block = jnp.concatenate(
                [own[r : r + 1, kk * LANES : (kk + 1) * LANES] for kk in range(levels)], 0
            )
            for p in range(copies):
                rows.append(block if p == 0 else jnp.roll(block, -p * features, axis=1))
        histograms[l] = jnp.concatenate(rows, 0).T[:features]


def exchange(value, axis, bit):
    count = lax.axis_size(axis)
    return lax.ppermute(value, axis, [(i, i ^ bit) for i in range(count)])


def shards(gradient, hessian, groups, leaf_ids, bins, group_sizes, variance_ratio):
    owners = lax.axis_size("rows")
    bits = [1 << n for n in range(owners.bit_length() - 1)]
    own_groups = group_sizes.shape[0]
    group_count = own_groups * owners
    features, row_count = bins.shape
    blocks = row_count // LANES
    copies = LANES // features
    levels = BINS // copies
    share = LEAVES // owners
    high_count = group_count // LANES
    vmem = pl.BlockSpec(memory_space=pltpu.VMEM)
    smem = pl.BlockSpec(memory_space=pltpu.SMEM)

    gradient = gradient.reshape(blocks, LANES)
    groups = groups.reshape(blocks, LANES)
    leaf_ids = leaf_ids.reshape(blocks, LANES)
    curve = hessian.astype(jnp.float32).reshape(blocks, LANES)

    message = pl.pallas_call(
        group_sum_kernel,
        out_shape=jax.ShapeDtypeStruct((2 * high_count, LANES), jnp.float32),
        in_specs=[vmem] * 3,
        out_specs=vmem,
        compiler_params=PARAMS,
        name="group_sum",
    )(gradient, groups, group_sizes.reshape(own_groups // LANES, LANES))

    turn_rows = min(2048, row_count)
    turned = pl.pallas_call(
        turn_kernel,
        grid=(row_count // turn_rows,),
        out_shape=jax.ShapeDtypeStruct((row_count, LANES), jnp.int8),
        in_specs=[pl.BlockSpec((features, turn_rows), lambda i: (0, i))],
        out_specs=pl.BlockSpec((turn_rows, LANES), lambda i: (i, 0)),
        compiler_params=PARAMS,
        name="turn_bins",
    )(bins)

    for bit in bits:
        message = message + exchange(message, "rows", bit)

    own_rows = own_groups // LANES
    begin = lax.axis_index("rows") * own_rows
    own_total = lax.dynamic_slice_in_dim(message, begin, own_rows, 0)
    own_size = lax.dynamic_slice_in_dim(message, high_count + begin, own_rows, 0)
    own_means = (-own_total / (own_size + variance_ratio[0])).reshape(own_groups)

    owner_order = [0]
    for bit in reversed(bits):
        owner_order = owner_order + [o | bit for o in owner_order]
    left, unscale = pl.pallas_call(
        functools.partial(weigh_kernel, owner_order),
        out_shape=(
            jax.ShapeDtypeStruct((4 * LEAVES, row_count), F8),
            jax.ShapeDtypeStruct((8, LANES), jnp.float32),
        ),
        in_specs=[vmem, smem, vmem, vmem, vmem, vmem],
        out_specs=(vmem, vmem),
        compiler_params=PARAMS,
        name="weigh_rows",
    )(message, variance_ratio, gradient, curve, groups, leaf_ids)

    level_step = 4
    chunks = 2
    chunk_levels = levels // chunks
    pieces = []
    for c in range(chunks):
        keep, send = pl.pallas_call(
            functools.partial(histogram_kernel, c * chunk_levels, level_step),
            grid=(chunk_levels // level_step,),
            out_shape=[jax.ShapeDtypeStruct((LEAVES, chunk_levels * LANES), jnp.float32)] * 2,
            in_specs=[
                pl.BlockSpec((row_count, LANES), lambda i: (0, 0)),
                pl.BlockSpec((4 * LEAVES, row_count), lambda i: (0, 0)),
                pl.BlockSpec((8, LANES), lambda i: (0, 0)),
            ],
            out_specs=[pl.BlockSpec((LEAVES, level_step * LANES), lambda i: (0, i))] * 2,
            compiler_params=PARAMS,
            name="histogram",
        )(turned, left, unscale)
        pieces.append((keep, send))
    done = []
    for keep, send in pieces:
        for n, bit in enumerate(bits):
            total = keep + exchange(send, "rows", bit)
            middle = total.shape[0] // 2
            keep, send = total[:middle], total[middle:]
        done.append(total)

    own = jnp.concatenate(done, 1)
    histograms = pl.pallas_call(
        arrange_kernel,
        out_shape=jax.ShapeDtypeStruct((share, features, 2 * BINS), jnp.float32),
        in_specs=[vmem],
        out_specs=vmem,
        compiler_params=PARAMS,
        name="arrange",
    )(own)
    return histograms, own_means


def solution(mesh):
    in_specs = (P("rows"), P("rows"), P("rows"), P("rows"), P("feat", "rows"), P("rows"), P())
    out_specs = (P("rows", "feat", None), P("rows"))
    return jax.shard_map(shards, mesh=mesh, in_specs=in_specs, out_specs=out_specs, check_vma=False)
```

time: 355 us -> 56.7 us (0.16)
  other arithmetic: 85.6 us -> 1.49 us
  blocking collectives: 82.1 us -> 0 us
  matrix products: 82 us -> 0 us
  waiting for transfers between devices: 59.1 us -> 16.7 us
  local copies, waits for them, and re-layouts: 27.9 us -> 2.39 us
  Pallas kernels: 0 us -> 20.1 us
  starting transfers between devices: 0.04 us -> 14.2 us
  between operations: 14.8 us -> 1.42 us
    dot_general x18 -> x0, matrix products: 82 us -> none  [the longest x8 69.1 us: advance(): lax.dot_general(left_side, right_side, (((1,), (1,)), ((), ())), preferre...]
    eq x8 -> x0, other arithmetic: 70.8 us -> none  [advance(): bin_block[:, None, :] == levels[None, :, None]]
    reduce_scatter x1 -> x0, waiting for transfers between devices: 59.1 us -> none  [shards(): lax.psum_scatter(hist_term(leaf_ids, (adjusted, hessian), bins, leaf_shar...]
    unnamed x1 -> x0, blocking collectives: 42.1 us -> none
    all_gather x1 -> x0, blocking collectives: 40 us -> none  [shards(): all_means = lax.all_gather(mean_share, ('rows', 'feat'), axis=0, tiled=True)]
    pallas_call x0 -> x6, Pallas kernels: none -> 20.1 us  [the longest x2 9.92 us: shards(): pl.pallas_call(functools.partial(histogram_kernel, c * chunk_levels, leve...]
    ppermute x0 -> x9, waiting for transfers between devices: none -> 16.7 us  [exchange(): return lax.ppermute(value, axis, [(i, i ^ bit) for i in range(count)])]
    dynamic_slice x29 -> x0, local copies, waits for them, and re-layouts: 16.5 us -> none  [the longest x8 8.67 us: advance(): bin_block = lax.dynamic_slice_in_dim(bin_rows, offset, block_rows, 1)]
  transfers between devices with their start and end apart: 1 -> 9, of which waited for: 1 -> 6; matrix products, arithmetic and copies ran while one was open for 0% -> 3% of each run, Pallas kernels for 0% -> 19%
where the time goes in v1:
time: 56.7 us; the launch traced here: 56.3 us
  Pallas kernels  20.1 us (35%)
  waiting for transfers between devices  16.7 us (29%)
  starting transfers between devices  14.2 us (25%)
  local copies, waits for them, and re-layouts  2.39 us (4%)
  other arithmetic  1.49 us (3%)
  between operations  1.42 us (3%)
    ppermute x9, waiting for transfers between devices, exchange(): return lax.ppermute(value, axis, [(i, i ^ bit) for i in range(count)])  16.7 us
    ppermute x9, starting transfers between devices, exchange(): return lax.ppermute(value, axis, [(i, i ^ bit) for i in range(count)])  14.2 us
    pallas_call x2, Pallas kernels, shards(): pl.pallas_call(functools.partial(histogram_kernel, c * chunk_levels, leve...  9.92 us
    pallas_call x1, Pallas kernels, shards(): pl.pallas_call(turn_kernel, grid=(row_count // turn_rows,), out_shape=jax...  6.02 us
    unnamed x8, local copies, waits for them, and re-layouts  2.36 us
    pallas_call x1, Pallas kernels, shards(): pl.pallas_call(functools.partial(weigh_kernel, owner_order), out_shape=(j...  1.86 us
    pallas_call x1, Pallas kernels, shards(): pl.pallas_call(group_sum_kernel, out_shape=jax.ShapeDtypeStruct((2 * high...  1.43 us
  transfers between devices with their start and end apart: 9, of which 6 were waited for; matrix products, arithmetic and copies ran while one was open for 3% of the time, Pallas kernels for 19%

profile of v1, /device:TPU:0, one launch (start us, length us, event | category | flops | bytes accessed | tf_op | source)
XLA Modules:
  0.0 56.3 jit_solution(18223847650852079955)
XLA Ops:
  0.6 0.8 %copy-done = f32[16384]{0:T(1024)S(1)} copy-done((f32[16384]{0:T(1024)S(1)}, f32[16384]{0:T(1024)}, u32[]{:S(2)}) %copy-start) | copy-done | bytes 65560
  1.5 0.8 %copy-done.1 = s32[16384]{0:T(1024)S(1)} copy-done((s32[16384]{0:T(1024)S(1)}, s32[16384]{0:T(1024)}, u32[]{:S(2)}) %copy-start.1) | copy-done | bytes 65560
  2.3 0.7 %copy-done.3 = s32[512]{0:T(512)S(1)} copy-done((s32[512]{0:T(512)S(1)}, s32[512]{0:T(512)}, u32[]{:S(2)}) %copy-start.3) | copy-done | bytes 2072
  3.0 1.4 %group_sum.1 = f32[64,128]{1,0:T(8,128)S(1)} custom-call(f32[128,128]{1,0:T(8,128)S(1)} %bitcast.11, s32[128,128]{1,0:T(8,128)S(1)} %bitcast.13, s32[4,128]{1,0:T(4,128)S(1)} %bitcast.16), custom_call_target="tpu_custom_call" | custom-call | tf_op jit(solution)/shard_map/group_sum/pallas_call | solution.py:179
  4.4 3.0 %collective-permute-start = (f32[64,128]{1,0:T(8,128)S(1)}, f32[64,128]{1,0:T(8,128)S(1)}, u32[]{:S(2)}, u32[]{:S(2)}) collective-permute-start(f32[64,128]{1,0:T(8,128)S(1)} %group_sum.1), channel_id=1, source_target_pairs={{0,4},{4,0},{8,12},{12,8},{16,20},{20,16},{24,28},{28,24},{1,5},{5... | collective-permute-start | bytes 98312 | tf_op jit(solution)/shard_map/ppermute | solution.py:157
  7.4 1.9 %collective-permute-done = f32[64,128]{1,0:T(8,128)S(1)} collective-permute-done((f32[64,128]{1,0:T(8,128)S(1)}, f32[64,128]{1,0:T(8,128)S(1)}, u32[]{:S(2)}, u32[]{:S(2)}) %collective-permute-start) | collective-permute-done | bytes 32800 | tf_op jit(solution)/shard_map/ppermute | solution.py:157
  9.3 2.1 %collective-permute-start.1 = (f32[64,128]{1,0:T(8,128)S(1)}, f32[64,128]{1,0:T(8,128)S(1)}, u32[]{:S(2)}, u32[]{:S(2)}) collective-permute-start(f32[64,128]{1,0:T(8,128)S(1)} %add.41), channel_id=1, source_target_pairs={{0,8},{4,12},{8,0},{12,4},{16,24},{20,28},{24,16},{28,20},{1,9},{5... | collective-permute-start | bytes 98312 | tf_op jit(solution)/shard_map/ppermute | solution.py:157
  11.4 1.9 %collective-permute-done.1 = f32[64,128]{1,0:T(8,128)S(1)} collective-permute-done((f32[64,128]{1,0:T(8,128)S(1)}, f32[64,128]{1,0:T(8,128)S(1)}, u32[]{:S(2)}, u32[]{:S(2)}) %collective-permute-start.1) | collective-permute-done | bytes 32800 | tf_op jit(solution)/shard_map/ppermute | solution.py:157
  13.3 3.0 %collective-permute-start.2 = (f32[64,128]{1,0:T(8,128)S(1)}, f32[64,128]{1,0:T(8,128)S(1)}, u32[]{:S(2)}, u32[]{:S(2)}) collective-permute-start(f32[64,128]{1,0:T(8,128)S(1)} %add.42), channel_id=1, source_target_pairs={{0,16},{4,20},{8,24},{12,28},{16,0},{20,4},{24,8},{28,12},{1,17},{... | collective-permute-start | bytes 98312 | tf_op jit(solution)/shard_map/ppermute | solution.py:157
  16.3 0.8 %bitcast_convert_fusion.hessian = f32[128,128]{1,0:T(8,128)S(1)} fusion(bf16[16384]{0:T(1024)(128)(2,1)} %param.8), kind=kLoop, calls=%fused_computation.5 | loop fusion | flops 16384 | bytes 98304 | tf_op jit(solution)/shard_map/reshape | solution.py:177
  17.1 6.0 %turn_bins.1.turned = s8[16384,128]{1,0:T(32,128)(4,1)S(1)} custom-call(s32[64,16384]{1,0:T(8,128)} %bins.1), custom_call_target="tpu_custom_call" | custom-call | tf_op jit(solution)/shard_map/turn_bins/pallas_call | solution.py:189
  23.8 1.9 %weigh_rows.1 = (f8e4m3fn[128,16384]{1,0:T(32,128)(4,1)S(1)}, f32[8,128]{1,0:T(8,128)S(1)}) custom-call(f32[64,128]{1,0:T(8,128)S(1)} %add.43.message, f32[1]{0:T(128)} %copy.9.ratio, f32[128,128]{1,0:T(8,128)S(1)} %bitcast.12, f32[128,128]{1,0:T(8,128)S(1)} %bitcast_convert_fusion.hessian, s32[128,128]{1,0:T(8,128)S(1)} %bitcast.14, s32[128,128]{1,0:T(8,128)S(1)} %bitcast.15), custom_call_target="tpu_custom_call" | custom-call | tf_op jit(solution)/shard_map/weigh_rows/pallas_call | solution.py:211
  25.7 5.0 %histogram.3 = (f32[32,2048]{1,0:T(8,128)S(1)}, f32[32,2048]{1,0:T(8,128)S(1)}) custom-call(s8[16384,128]{1,0:T(32,128)(4,1)S(1)} %turn_bins.1.turned, f8e4m3fn[128,16384]{1,0:T(32,128)(4,1)S(1)} %get-tuple-element.8.left, f32[8,128]{1,0:T(8,128)S(1)} %get-tuple-element.9.unscale), custom_call_target="tpu_custom_call" | custom-call | tf_op jit(solution)/shard_map/histogram/pallas_call | solution.py:228
  30.6 1.6 %collective-permute-start.6 = (f32[32,2048]{1,0:T(8,128)S(1)}, f32[32,2048]{1,0:T(8,128)S(1)}, u32[]{:S(2)}, u32[]{:S(2)}) collective-permute-start(f32[32,2048]{1,0:T(8,128)S(1)} %get-tuple-element.13), channel_id=1, source_target_pairs={{0,4},{4,0},{8,12},{12,8},{16,20},{20,16},{24,28},{28,24},{1,5},{5... | collective-permute-start | bytes 786440 | tf_op jit(solution)/shard_map/ppermute | solution.py:157
  32.2 5.0 %histogram.2 = (f32[32,2048]{1,0:T(8,128)S(1)}, f32[32,2048]{1,0:T(8,128)S(1)}) custom-call(s8[16384,128]{1,0:T(32,128)(4,1)S(1)} %turn_bins.1.turned, f8e4m3fn[128,16384]{1,0:T(32,128)(4,1)S(1)} %get-tuple-element.8.left, f32[8,128]{1,0:T(8,128)S(1)} %get-tuple-element.9.unscale), custom_call_target="tpu_custom_call" | custom-call | tf_op jit(solution)/shard_map/histogram/pallas_call | solution.py:228
  37.2 0.6 %collective-permute-start.3 = (f32[32,2048]{1,0:T(8,128)S(1)}, f32[32,2048]{1,0:T(8,128)S(1)}, u32[]{:S(2)}, u32[]{:S(2)}) collective-permute-start(f32[32,2048]{1,0:T(8,128)S(1)} %get-tuple-element.11), channel_id=1, source_target_pairs={{0,4},{4,0},{8,12},{12,8},{16,20},{20,16},{24,28},{28,24},{1,5},{5... | collective-permute-start | bytes 786440 | tf_op jit(solution)/shard_map/ppermute | solution.py:157
  37.8 1.6 %collective-permute-start.7 = (f32[16,2048]{1,0:T(8,128)S(1)}, f32[16,2048]{1,0:T(8,128)S(1)}, u32[]{:S(2)}, u32[]{:S(2)}) collective-permute-start(f32[16,2048]{1,0:T(8,128)S(1)} %slice.37), channel_id=1, source_target_pairs={{0,8},{4,12},{8,0},{12,4},{16,24},{20,28},{24,16},{28,20},{1,9},{5... | collective-permute-start | bytes 393224 | tf_op jit(solution)/shard_map/ppermute | solution.py:157
  39.5 0.6 %fusion = f32[512]{0:T(512)} fusion(f32[64,128]{1,0:T(8,128)S(1)} %add.43.message, s32[]{:T(128)S(6)} %select_n.7, s32[]{:T(128)S(6)} %select_n.6, f32[]{:T(128)} %bitcast.10), kind=kLoop, calls=%fused_computation.7 | loop fusion | flops 1536 | bytes 6156 | tf_op jit(solution)/shard_map/reshape | solution.py:206
  40.0 3.6 %collective-permute-done.3 = f32[32,2048]{1,0:T(8,128)S(1)} collective-permute-done((f32[32,2048]{1,0:T(8,128)S(1)}, f32[32,2048]{1,0:T(8,128)S(1)}, u32[]{:S(2)}, u32[]{:S(2)}) %collective-permute-start.3) | collective-permute-done | bytes 262176 | tf_op jit(solution)/shard_map/ppermute | solution.py:157
  43.7 1.6 %collective-permute-start.4 = (f32[16,2048]{1,0:T(8,128)S(1)}, f32[16,2048]{1,0:T(8,128)S(1)}, u32[]{:S(2)}, u32[]{:S(2)}) collective-permute-start(f32[16,2048]{1,0:T(8,128)S(1)} %slice.33), channel_id=1, source_target_pairs={{0,8},{4,12},{8,0},{12,4},{16,24},{20,28},{24,16},{28,20},{1,9},{5... | collective-permute-start | bytes 393224 | tf_op jit(solution)/shard_map/ppermute | solution.py:157
  45.8 3.7 %collective-permute-done.4 = f32[16,2048]{1,0:T(8,128)S(1)} collective-permute-done((f32[16,2048]{1,0:T(8,128)S(1)}, f32[16,2048]{1,0:T(8,128)S(1)}, u32[]{:S(2)}, u32[]{:S(2)}) %collective-permute-start.4) | collective-permute-done | bytes 131104 | tf_op jit(solution)/shard_map/ppermute | solution.py:157
  49.7 1.5 %collective-permute-done.8 = f32[8,2048]{1,0:T(8,128)S(1)} collective-permute-done((f32[8,2048]{1,0:T(8,128)S(1)}, f32[8,2048]{1,0:T(8,128)S(1)}, u32[]{:S(2)}, u32[]{:S(2)}) %collective-permute-start.8) | collective-permute-done | bytes 65568 | tf_op jit(solution)/shard_map/ppermute | solution.py:157
  51.2 4.2 %collective-permute-done.5 = f32[8,2048]{1,0:T(8,128)S(1)} collective-permute-done((f32[8,2048]{1,0:T(8,128)S(1)}, f32[8,2048]{1,0:T(8,128)S(1)}, u32[]{:S(2)}, u32[]{:S(2)}) %collective-permute-start.5) | collective-permute-done | bytes 65568 | tf_op jit(solution)/shard_map/ppermute | solution.py:157
  55.4 0.8 %arrange.1 = f32[4,64,128]{2,1,0:T(8,128)} custom-call(f32[8,4096]{1,0:T(8,128)S(1)} %pad_maximum_fusion.own), custom_call_target="tpu_custom_call" | custom-call | tf_op jit(solution)/shard_map/arrange/pallas_call | solution.py:251
  (24 shorter events, 0.8 us)
Async XLA Ops:
  0.6 0.8 %copy-start = (f32[16384]{0:T(1024)S(1)}, f32[16384]{0:T(1024)}, u32[]{:S(2)}) copy-start(f32[16384]{0:T(1024)} %param.7) | copy-start | bytes 196612
  1.5 0.8 %copy-start.1 = (s32[16384]{0:T(1024)S(1)}, s32[16384]{0:T(1024)}, u32[]{:S(2)}) copy-start(s32[16384]{0:T(1024)} %param.9) | copy-start | bytes 196612
  2.3 0.7 %copy-start.3 = (s32[512]{0:T(512)S(1)}, s32[512]{0:T(512)}, u32[]{:S(2)}) copy-start(s32[512]{0:T(512)} %param.12) | copy-start | bytes 6148
  4.4 4.9 %collective-permute-start = (f32[64,128]{1,0:T(8,128)S(1)}, f32[64,128]{1,0:T(8,128)S(1)}, u32[]{:S(2)}, u32[]{:S(2)}) collective-permute-start(f32[64,128]{1,0:T(8,128)S(1)} %group_sum.1), channel_id=1, source_target_pairs={{0,4},{4,0},{8,12},{12,8},{16,20},{20,16},{24,28},{28,24},{1,5},{5... | collective-permute-start | bytes 98312 | tf_op jit(solution)/shard_map/ppermute | solution.py:157
  9.3 4.0 %collective-permute-start.1 = (f32[64,128]{1,0:T(8,128)S(1)}, f32[64,128]{1,0:T(8,128)S(1)}, u32[]{:S(2)}, u32[]{:S(2)}) collective-permute-start(f32[64,128]{1,0:T(8,128)S(1)} %add.41), channel_id=1, source_target_pairs={{0,8},{4,12},{8,0},{12,4},{16,24},{20,28},{24,16},{28,20},{1,9},{5... | collective-permute-start | bytes 98312 | tf_op jit(solution)/shard_map/ppermute | solution.py:157
  13.3 10.5 %collective-permute-start.2 = (f32[64,128]{1,0:T(8,128)S(1)}, f32[64,128]{1,0:T(8,128)S(1)}, u32[]{:S(2)}, u32[]{:S(2)}) collective-permute-start(f32[64,128]{1,0:T(8,128)S(1)} %add.42), channel_id=1, source_target_pairs={{0,16},{4,20},{8,24},{12,28},{16,0},{20,4},{24,8},{28,12},{1,17},{... | collective-permute-start | bytes 98312 | tf_op jit(solution)/shard_map/ppermute | solution.py:157
  17.1 6.7 %copy-start.2 = (s32[16384]{0:T(1024)S(1)}, s32[16384]{0:T(1024)}, u32[]{:S(2)}) copy-start(s32[16384]{0:T(1024)} %param.10) | copy-start | bytes 196612
  30.6 7.1 %collective-permute-start.6 = (f32[32,2048]{1,0:T(8,128)S(1)}, f32[32,2048]{1,0:T(8,128)S(1)}, u32[]{:S(2)}, u32[]{:S(2)}) collective-permute-start(f32[32,2048]{1,0:T(8,128)S(1)} %get-tuple-element.13), channel_id=1, source_target_pairs={{0,4},{4,0},{8,12},{12,8},{16,20},{20,16},{24,28},{28,24},{1,5},{5... | collective-permute-start | bytes 786440 | tf_op jit(solution)/shard_map/ppermute | solution.py:157
  37.2 6.4 %collective-permute-start.3 = (f32[32,2048]{1,0:T(8,128)S(1)}, f32[32,2048]{1,0:T(8,128)S(1)}, u32[]{:S(2)}, u32[]{:S(2)}) collective-permute-start(f32[32,2048]{1,0:T(8,128)S(1)} %get-tuple-element.11), channel_id=1, source_target_pairs={{0,4},{4,0},{8,12},{12,8},{16,20},{20,16},{24,28},{28,24},{1,5},{5... | collective-permute-start | bytes 786440 | tf_op jit(solution)/shard_map/ppermute | solution.py:157
  37.8 7.5 %collective-permute-start.7 = (f32[16,2048]{1,0:T(8,128)S(1)}, f32[16,2048]{1,0:T(8,128)S(1)}, u32[]{:S(2)}, u32[]{:S(2)}) collective-permute-start(f32[16,2048]{1,0:T(8,128)S(1)} %slice.37), channel_id=1, source_target_pairs={{0,8},{4,12},{8,0},{12,4},{16,24},{20,28},{24,16},{28,20},{1,9},{5... | collective-permute-start | bytes 393224 | tf_op jit(solution)/shard_map/ppermute | solution.py:157
  43.7 5.7 %collective-permute-start.4 = (f32[16,2048]{1,0:T(8,128)S(1)}, f32[16,2048]{1,0:T(8,128)S(1)}, u32[]{:S(2)}, u32[]{:S(2)}) collective-permute-start(f32[16,2048]{1,0:T(8,128)S(1)} %slice.33), channel_id=1, source_target_pairs={{0,8},{4,12},{8,0},{12,4},{16,24},{20,28},{24,16},{28,20},{1,9},{5... | collective-permute-start | bytes 393224 | tf_op jit(solution)/shard_map/ppermute | solution.py:157
  45.4 5.8 %collective-permute-start.8 = (f32[8,2048]{1,0:T(8,128)S(1)}, f32[8,2048]{1,0:T(8,128)S(1)}, u32[]{:S(2)}, u32[]{:S(2)}) collective-permute-start(f32[8,2048]{1,0:T(8,128)S(1)} %slice.39), channel_id=1, source_target_pairs={{0,16},{4,20},{8,24},{12,28},{16,0},{20,4},{24,8},{28,12},{1,17},{... | collective-permute-start | bytes 196616 | tf_op jit(solution)/shard_map/ppermute | solution.py:157
  49.4 5.9 %collective-permute-start.5 = (f32[8,2048]{1,0:T(8,128)S(1)}, f32[8,2048]{1,0:T(8,128)S(1)}, u32[]{:S(2)}, u32[]{:S(2)}) collective-permute-start(f32[8,2048]{1,0:T(8,128)S(1)} %slice.35), channel_id=1, source_target_pairs={{0,16},{4,20},{8,24},{12,28},{16,0},{20,4},{24,8},{28,12},{1,17},{... | collective-permute-start | bytes 196616 | tf_op jit(solution)/shard_map/ppermute | solution.py:157

commit v2 on v1

v2 whole, which is shorter than its diff:
```python
import functools
import math

import jax
import jax.numpy as jnp
from jax import lax
from jax.experimental import pallas as pl
from jax.experimental.pallas import tpu as pltpu
from jax.sharding import PartitionSpec as P

BINS = 64
LEAVES = 32
LANES = 128
TERMS = 6
TGRANT = 48
K1_STEP = 32
GRANT = 60
WEIGHT = 8
CHUNKS = 2
F8 = jnp.float8_e4m3fn
STREAM = pltpu.CompilerParams(vmem_limit_bytes=int(GRANT * 2**20))
PARAMS = pltpu.CompilerParams(vmem_limit_bytes=48 * 2**20)


def group_sum_kernel(gradient, groups, sizes, message):
    blocks = gradient.shape[0]
    own = sizes.shape[0]
    high_count = message.shape[0] - own
    rest, parts = gradient[...], []
    for n in range(TERMS):
        part = rest.astype(F8).astype(jnp.float32)
        rest = (rest - part) * 16.0
        parts.append(part)
    ids = groups[...]
    high, low = lax.shift_right_logical(ids, 7), ids & (LANES - 1)
    high_levels = lax.broadcasted_iota(jnp.int32, (high_count, LANES), 0).astype(jnp.int8)
    low_levels = lax.broadcasted_iota(jnp.int32, (LANES, LANES), 0).astype(jnp.int8)
    zero, one = jnp.zeros((), F8), jnp.ones((), F8)

    def spread(values, j, rows, dtype):
        return jnp.broadcast_to(values[j : j + 1], (rows, LANES)).astype(dtype)

    total = jnp.zeros((TERMS * high_count, LANES), jnp.float32)
    step = min(K1_STEP, blocks)
    for start in range(0, blocks, step):
        left, right = [], []
        for j in range(start, start + step):
            here = spread(high, j, high_count, jnp.int8) == high_levels
            left.append(
                jnp.concatenate(
                    [jnp.where(here, spread(part, j, high_count, F8), zero) for part in parts], 0
                )
            )
            right.append(jnp.where(spread(low, j, LANES, jnp.int8) == low_levels, one, zero))
        total += lax.dot_general(
            jnp.concatenate(left, 1),
            jnp.concatenate(right, 1),
            (((1,), (1,)), ((), ())),
            preferred_element_type=jnp.float32,
        )
    result = total[(TERMS - 1) * high_count :]
    for n in reversed(range(TERMS - 1)):
        result = result * 0.0625 + total[n * high_count : (n + 1) * high_count]
    message[:high_count] = result
    message[high_count:] = sizes[...].astype(jnp.float32)


def turn_kernel(bins, turned):
    features, rows = bins.shape
    copies = LANES // features
    levels = BINS // copies
    for start in range(0, rows, LANES):
        block = bins[:, start : start + LANES]
        stack = jnp.concatenate([block - p * levels for p in range(copies)], 0)
        turned[start : start + LANES] = stack.astype(jnp.int8).T


def weigh_kernel(owner_order, message, ratio, gradient, hessian, groups, leaf_ids, left, unscale):
    blocks = gradient.shape[0]
    high_count = message.shape[0] // 2
    me = lax.axis_index("rows")
    owners = len(owner_order)
    share = LEAVES // owners
    own = high_count // owners
    size_of = jnp.concatenate(
        [message[pl.ds(high_count + (me ^ o) * own, own)] for o in range(owners)], 0
    )
    means = -message[:high_count] / (size_of + ratio[0])
    ids = groups[...]
    high, low = lax.shift_right_logical(ids, 7), ids & (LANES - 1)
    found = []
    for j in range(0, blocks, 8):
        low_here, high_here = low[j : j + 8], high[j : j + 8]
        value = jnp.zeros((8, LANES), jnp.float32)
        for h in range(high_count):
            row = jnp.broadcast_to(means[h : h + 1], (8, LANES))
            picked = jnp.take_along_axis(row, low_here, axis=1, mode="promise_in_bounds")
            value = jnp.where(high_here == h, picked, value)
        found.append(value)
    row_means = jnp.concatenate(found, 0)
    curve = hessian[...].astype(jnp.float32)
    adjusted = (gradient[...] + curve * row_means).astype(jnp.bfloat16).astype(jnp.float32)

    level = jnp.max(jnp.abs(adjusted)) * 32.0
    scale, back = jnp.float32(32.0), jnp.float32(1.0 / 32.0)
    for power in (16, 8, 4, 2, 1):
        big = level > 256.0 * 2.0 ** (power - 1)
        level = jnp.where(big, level * 2.0**-power, level)
        scale = jnp.where(big, scale * 2.0**-power, scale)
        back = jnp.where(big, back * 2.0**power, back)
    unscale[...] = jnp.full(unscale.shape, back, jnp.float32)

    scaled = adjusted * scale
    adjusted_high = scaled.astype(F8).astype(jnp.float32)
    adjusted_low = (scaled - adjusted_high) * 16.0
    curve_high = curve.astype(F8).astype(jnp.float32)
    curve_low = (curve - curve_high) * 16.0

    half = 2 * LEAVES
    row = lax.broadcasted_iota(jnp.int32, (half, LANES), 0)
    place = row // (2 * share)
    owner = jnp.zeros_like(place)
    for position, other in enumerate(owner_order):
        owner = jnp.where(place == position, other, owner)
    leaf_of = (owner ^ me) * share + (row % (2 * share)) // 2
    leaf_of = leaf_of.astype(jnp.int8)
    is_gradient = (row[:LEAVES] % 2).astype(jnp.int8) == jnp.zeros((), jnp.int8)
    leaves = leaf_ids[...]
    zero = jnp.zeros((), F8)

    def spread(values, j, dtype):
        return jnp.broadcast_to(values[j : j + 1], (LEAVES, LANES)).astype(dtype)

    for j in range(blocks):
        leaf = spread(leaves, j, jnp.int8)
        members = [leaf == leaf_of[:LEAVES], leaf == leaf_of[LEAVES:]]
        parts = []
        for one, two in ((adjusted_high, curve_high), (adjusted_low, curve_low)):
            both = jnp.where(is_gradient, spread(one, j, F8), spread(two, j, F8))
            parts += [jnp.where(member, both, zero) for member in members]
        left[:, j * LANES : (j + 1) * LANES] = jnp.concatenate(parts, 0)


def histogram_kernel(level_step, turned, left, unscale, keep, send):
    base = pl.program_id(0) * level_step
    bins = turned[...]
    hot = []
    for q in range(level_step):
        level = (base + q).astype(jnp.int8)
        hot.append(jnp.where(bins == level, jnp.ones((), F8), jnp.zeros((), F8)))
    both = jnp.dot(left[...], jnp.concatenate(hot, 1), preferred_element_type=jnp.float32)
    half = both.shape[0] // 2
    total = both[:half] + both[half:] * 0.0625
    is_gradient = lax.broadcasted_iota(jnp.int32, (half, 1), 0) % 2 == 0
    total = total * jnp.where(is_gradient, unscale[0:1, 0:1], 1.0)
    keep[...] = total[: half // 2]
    send[...] = total[half // 2 :]


def arrange_kernel(*refs):
    *parts, histograms = refs
    share, features, _ = histograms.shape
    width = features // len(parts)
    copies = LANES // width
    levels = BINS // copies
    for c, own in enumerate(parts):
        for l in range(share):
            rows = []
            for channel in range(2):
                r = 2 * l + channel
                block = jnp.concatenate(
                    [own[r : r + 1, kk * LANES : (kk + 1) * LANES] for kk in range(levels)], 0
                )
                for p in range(copies):
                    rows.append(block if p == 0 else jnp.roll(block, -p * width, axis=1))
            histograms[l, c * width : (c + 1) * width] = jnp.concatenate(rows, 0).T[:width]


def exchange(value, axis, bit):
    count = lax.axis_size(axis)
    return lax.ppermute(value, axis, [(i, i ^ bit) for i in range(count)])


def shards(gradient, hessian, groups, leaf_ids, bins, group_sizes, variance_ratio):
    owners = lax.axis_size("rows")
    bits = [1 << n for n in range(owners.bit_length() - 1)]
    own_groups = group_sizes.shape[0]
    group_count = own_groups * owners
    features, row_count = bins.shape
    blocks = row_count // LANES
    width = features // CHUNKS
    copies = LANES // width
    levels = BINS // copies
    share = LEAVES // owners
    high_count = group_count // LANES
    vmem = pl.BlockSpec(memory_space=pltpu.VMEM)
    smem = pl.BlockSpec(memory_space=pltpu.SMEM)

    gradient = gradient.reshape(blocks, LANES)
    groups = groups.reshape(blocks, LANES)
    leaf_ids = leaf_ids.reshape(blocks, LANES)
    curve = hessian.astype(jnp.float32).reshape(blocks, LANES)

    whole = lambda array: pl.BlockSpec(array.shape, lambda i: (0,) * array.ndim)
    own_rows = own_groups // LANES
    sizes = group_sizes.reshape(own_rows, LANES)
    message = pl.pallas_call(
        group_sum_kernel,
        grid=(1,),
        out_shape=jax.ShapeDtypeStruct((high_count + own_rows, LANES), jnp.float32),
        in_specs=[whole(gradient), whole(groups), whole(sizes)],
        out_specs=vmem,
        compiler_params=STREAM,
        name="group_sum",
    )(gradient, groups, sizes)

    def turn(bins):
        return pl.pallas_call(
            turn_kernel,
            out_shape=jax.ShapeDtypeStruct((row_count, LANES), jnp.int8),
            in_specs=[vmem],
            out_specs=vmem,
            compiler_params=pltpu.CompilerParams(vmem_limit_bytes=TGRANT * 2**20),
            cost_estimate=pl.CostEstimate(flops=0, bytes_accessed=4 * bins.size, transcendentals=0),
            name="turn_bins",
        )(bins)

    turned = []
    for n, bit in enumerate(bits):
        other = exchange(message, "rows", bit)
        if n < CHUNKS:
            turned.append(turn(bins[n * width : (n + 1) * width]))
        totals = message[:high_count] + other[:high_count]
        message = jnp.concatenate([totals, message[high_count:], other[high_count:]], 0)
        if n < CHUNKS:
            message, bins, turned = lax.optimization_barrier((message, bins, turned))

    own_total = lax.dynamic_slice_in_dim(message, lax.axis_index("rows") * own_rows, own_rows, 0)
    own_size = message[high_count : high_count + own_rows]
    own_means = (-own_total / (own_size + variance_ratio[0])).reshape(own_groups)

    owner_order = [0]
    for bit in reversed(bits):
        owner_order = owner_order + [o | bit for o in owner_order]
    left, unscale = pl.pallas_call(
        functools.partial(weigh_kernel, owner_order),
        out_shape=(
            jax.ShapeDtypeStruct((4 * LEAVES, row_count), F8),
            jax.ShapeDtypeStruct((8, LANES), jnp.float32),
        ),
        in_specs=[vmem, smem, vmem, vmem, vmem, vmem],
        out_specs=(vmem, vmem),
        compiler_params=PARAMS,
        name="weigh_rows",
    )(message, variance_ratio, gradient, curve, groups, leaf_ids)

    level_step = math.gcd(levels, 4)
    pieces = []
    for part in turned:
        pieces.append(
            pl.pallas_call(
                functools.partial(histogram_kernel, level_step),
                grid=(levels // level_step,),
                out_shape=[jax.ShapeDtypeStruct((LEAVES, levels * LANES), jnp.float32)] * 2,
                in_specs=[whole(part), whole(left), whole(unscale)],
                out_specs=[pl.BlockSpec((LEAVES, level_step * LANES), lambda i: (0, i))] * 2,
                compiler_params=PARAMS,
                cost_estimate=pl.CostEstimate(
                    flops=WEIGHT * LEAVES * levels * LANES * row_count, bytes_accessed=0, transcendentals=0
                ),
                name="histogram",
            )(part, left, unscale)
        )
    done = []
    for keep, send in pieces:
        for bit in bits:
            total = keep + exchange(send, "rows", bit)
            middle = total.shape[0] // 2
            keep, send = total[:middle], total[middle:]
        done.append(total)

    histograms = pl.pallas_call(
        arrange_kernel,
        out_shape=jax.ShapeDtypeStruct((share, features, 2 * BINS), jnp.float32),
        in_specs=[vmem] * len(done),
        out_specs=vmem,
        compiler_params=PARAMS,
        name="arrange",
    )(*done)
    return histograms, own_means


def solution(mesh):
    in_specs = (P("rows"), P("rows"), P("rows"), P("rows"), P("feat", "rows"), P("rows"), P())
    out_specs = (P("rows", "feat", None), P("rows"))
    return jax.shard_map(shards, mesh=mesh, in_specs=in_specs, out_specs=out_specs, check_vma=False)
```

time: 56.7 us -> 48 us (0.85)
  waiting for transfers between devices: 16.7 us -> 8.9 us
  Pallas kernels: 20.1 us -> 15.8 us
  starting transfers between devices: 14.2 us -> 18.2 us
  other arithmetic: 1.49 us -> 0.73 us
    ppermute x9, waiting for transfers between devices: 16.7 us -> 8.9 us  [exchange(): return lax.ppermute(value, axis, [(i, i ^ bit) for i in range(count)])]
    ppermute x9, starting transfers between devices: 14.2 us -> 18.2 us  [exchange(): return lax.ppermute(value, axis, [(i, i ^ bit) for i in range(count)])]
    pallas_call x4 -> x5, Pallas kernels: 17.4 us -> 13.6 us  [the longest x2 9.92 us: shards(): pl.pallas_call(functools.partial(histogram_kernel, level_step), grid=(lev...]
    slice x0 -> x8, local copies, waits for them, and re-layouts: none -> 2.6 us  [the longest x2 1.87 us: shards(): turned.append(turn(bins[n * width:(n + 1) * width]))]
    unnamed x8 -> x12, local copies, waits for them, and re-layouts: 2.36 us -> 0.04 us
    reshape x1, other arithmetic: 0.76 us -> 0.01 us  [shards(): curve = hessian.astype(jnp.float32).reshape(blocks, LANES)]
    pallas_call x1, Pallas kernels: 1.86 us -> 1.22 us  [shards(): pl.pallas_call(functools.partial(weigh_kernel, owner_order), out_shape=(j...]
  transfers between devices with their start and end apart: 9 -> 9, of which waited for: 6 -> 6; matrix products, arithmetic and copies ran while one was open for 3% -> 7% of each run, Pallas kernels for 19% -> 13%
where the time goes in v2:
time: 48 us; the launch traced here: 47.8 us
  starting transfers between devices  18.2 us (38%)
  Pallas kernels  15.8 us (33%)
  waiting for transfers between devices  8.9 us (19%)
  local copies, waits for them, and re-layouts  2.67 us (6%)
  between operations  1.49 us (3%)
  other arithmetic  0.73 us (2%)
    ppermute x9, starting transfers between devices, exchange(): return lax.ppermute(value, axis, [(i, i ^ bit) for i in range(count)])  18.2 us
    pallas_call x2, Pallas kernels, shards(): pl.pallas_call(functools.partial(histogram_kernel, level_step), grid=(lev...  9.92 us
    ppermute x9, waiting for transfers between devices, exchange(): return lax.ppermute(value, axis, [(i, i ^ bit) for i in range(count)])  8.9 us
    pallas_call x1, Pallas kernels, shards(): pl.pallas_call(group_sum_kernel, grid=(1,), out_shape=jax.ShapeDtypeStruc...  2.47 us
    slice x2, local copies, waits for them, and re-layouts, shards(): turned.append(turn(bins[n * width:(n + 1) * width]))  1.87 us
    pallas_call x1, Pallas kernels, shards(): pl.pallas_call(functools.partial(weigh_kernel, owner_order), out_shape=(j...  1.22 us
    pallas_call x2, Pallas kernels, turn(): pl.pallas_call(turn_kernel, out_shape=jax.ShapeDtypeStruct((row_count, LA...  1.21 us
    pallas_call x1, Pallas kernels, shards(): pl.pallas_call(arrange_kernel, out_shape=jax.ShapeDtypeStruct((share, fea...  0.96 us
  transfers between devices with their start and end apart: 9, of which 6 were waited for; matrix products, arithmetic and copies ran while one was open for 7% of the time, Pallas kernels for 13%

profile of v2, /device:TPU:0, one launch (start us, length us, event | category | flops | bytes accessed | tf_op | source)
XLA Modules:
  0.0 47.8 jit_solution(2407022131004861050)
XLA Ops:
  0.6 2.5 %group_sum.1 = f32[36,128]{1,0:T(8,128)} custom-call(f32[128,128]{1,0:T(8,128)} %bitcast.11, s32[128,128]{1,0:T(8,128)} %bitcast.13, s32[4,128]{1,0:T(4,128)} %bitcast.16), custom_call_target="tpu_custom_call" | custom-call | tf_op jit(solution)/shard_map/group_sum/pallas_call | solution.py:207
  3.1 3.0 %collective-permute-start = (f32[36,128]{1,0:T(8,128)}, f32[36,128]{1,0:T(8,128)S(1)}, u32[]{:S(2)}, u32[]{:S(2)}) collective-permute-start(f32[36,128]{1,0:T(8,128)} %group_sum.1), channel_id=1, source_target_pairs={{0,4},{4,0},{8,12},{12,8},{16,20},{20,16},{24,28},{28,24},{1,5},{5... | collective-permute-start | bytes 55304 | tf_op jit(solution)/shard_map/ppermute | solution.py:181
  6.1 0.7 %slice.95 = f32[4,128]{1,0:T(4,128)S(1)} slice(f32[36,128]{1,0:T(8,128)} %group_sum.1), slice={[32:36], [0:128]} | slice | bytes 4096 | tf_op jit(solution)/shard_map/slice | solution.py:234
  6.8 1.7 %slice.74.bins = s32[32,16384]{1,0:T(8,128)S(1)} slice(s32[64,16384]{1,0:T(8,128)} %param.11), slice={[0:32], [0:16384]} | slice | bytes 4194304 | tf_op jit(solution)/shard_map/slice | solution.py:232
  8.5 0.6 %turn_bins.2.turned = s8[16384,128]{1,0:T(32,128)(4,1)S(1)} custom-call(s32[32,16384]{1,0:T(8,128)S(1)} %slice.74.bins), custom_call_target="tpu_custom_call" | custom-call | bytes 2097152 | tf_op jit(solution)/shard_map/turn_bins/pallas_call | solution.py:218
  9.2 1.6 %collective-permute-start.1 = (f32[40,128]{1,0:T(8,128)S(1)}, f32[40,128]{1,0:T(8,128)S(1)}, u32[]{:S(2)}, u32[]{:S(2)}) collective-permute-start(f32[40,128]{1,0:T(8,128)S(1)} %pad_maximum_fusion.2), channel_id=1, source_target_pairs={{0,8},{4,12},{8,0},{12,4},{16,24},{20,28},{24,16},{28,20},{1,9},{5... | collective-permute-start | bytes 61448 | tf_op jit(solution)/shard_map/ppermute | solution.py:181
  11.0 0.6 %turn_bins.3.turned = s8[16384,128]{1,0:T(32,128)(4,1)S(1)} custom-call(s32[32,16384]{1,0:T(8,128)S(1)} %slice.79.bins), custom_call_target="tpu_custom_call" | custom-call | bytes 2097152 | tf_op jit(solution)/shard_map/turn_bins/pallas_call | solution.py:218
  11.6 1.4 %collective-permute-done.1 = f32[40,128]{1,0:T(8,128)S(1)} collective-permute-done((f32[40,128]{1,0:T(8,128)S(1)}, f32[40,128]{1,0:T(8,128)S(1)}, u32[]{:S(2)}, u32[]{:S(2)}) %collective-permute-start.1) | collective-permute-done | bytes 20512 | tf_op jit(solution)/shard_map/ppermute | solution.py:181
  13.1 2.7 %collective-permute-start.2 = (f32[48,128]{1,0:T(8,128)S(1)}, f32[48,128]{1,0:T(8,128)S(1)}, u32[]{:S(2)}, u32[]{:S(2)}) collective-permute-start(f32[48,128]{1,0:T(8,128)S(1)} %pad_maximum_fusion.1), channel_id=1, source_target_pairs={{0,16},{4,20},{8,24},{12,28},{16,0},{20,4},{24,8},{28,12},{1,17},{... | collective-permute-start | bytes 73736 | tf_op jit(solution)/shard_map/ppermute | solution.py:181
  16.4 1.5 %collective-permute-done.2 = f32[48,128]{1,0:T(8,128)S(1)} collective-permute-done((f32[48,128]{1,0:T(8,128)S(1)}, f32[48,128]{1,0:T(8,128)S(1)}, u32[]{:S(2)}, u32[]{:S(2)}) %collective-permute-start.2) | collective-permute-done | bytes 24608 | tf_op jit(solution)/shard_map/ppermute | solution.py:181
  17.9 1.2 %weigh_rows.1 = (f8e4m3fn[128,16384]{1,0:T(32,128)(4,1)S(1)}, f32[8,128]{1,0:T(8,128)S(1)}) custom-call(f32[64,128]{1,0:T(8,128)S(1)} %pad_maximum_fusion.message, f32[1]{0:T(128)} %copy.9.ratio, f32[128,128]{1,0:T(8,128)S(1)} %bitcast.12, f32[128,128]{1,0:T(8,128)S(1)} %bitcast_convert_fusion.hessian, s32[128,128]{1,0:T(8,128)S(1)} %bitcast.14, ...), custom_call_target="tpu_custom_call" | custom-call | tf_op jit(solution)/shard_map/weigh_rows/pallas_call | solution.py:245
  19.1 5.0 %histogram.3 = (f32[32,2048]{1,0:T(8,128)S(1)}, f32[32,2048]{1,0:T(8,128)S(1)}) custom-call(s8[16384,128]{1,0:T(32,128)(4,1)S(1)} %turn_bins.3.turned, f8e4m3fn[128,16384]{1,0:T(32,128)(4,1)S(1)} %get-tuple-element.19.left, f32[8,128]{1,0:T(8,128)S(1)} %get-tuple-element.20.unscale), custom_call_target="tpu_custom_call" | custom-call | flops 8589934592 | tf_op jit(solution)/shard_map/histogram/pallas_call | solution.py:261
  24.1 1.0 %collective-permute-start.6 = (f32[32,2048]{1,0:T(8,128)S(1)}, f32[32,2048]{1,0:T(8,128)S(1)}, u32[]{:S(2)}, u32[]{:S(2)}) collective-permute-start(f32[32,2048]{1,0:T(8,128)S(1)} %get-tuple-element.25), channel_id=1, source_target_pairs={{0,4},{4,0},{8,12},{12,8},{16,20},{20,16},{24,28},{28,24},{1,5},{5... | collective-permute-start | bytes 786440 | tf_op jit(solution)/shard_map/ppermute | solution.py:181
  25.1 5.0 %histogram.2 = (f32[32,2048]{1,0:T(8,128)S(1)}, f32[32,2048]{1,0:T(8,128)S(1)}) custom-call(s8[16384,128]{1,0:T(32,128)(4,1)S(1)} %turn_bins.2.turned, f8e4m3fn[128,16384]{1,0:T(32,128)(4,1)S(1)} %get-tuple-element.19.left, f32[8,128]{1,0:T(8,128)S(1)} %get-tuple-element.20.unscale), custom_call_target="tpu_custom_call" | custom-call | flops 8589934592 | tf_op jit(solution)/shard_map/histogram/pallas_call | solution.py:261
  30.0 1.2 %collective-permute-start.3 = (f32[32,2048]{1,0:T(8,128)S(1)}, f32[32,2048]{1,0:T(8,128)S(1)}, u32[]{:S(2)}, u32[]{:S(2)}) collective-permute-start(f32[32,2048]{1,0:T(8,128)S(1)} %get-tuple-element.22), channel_id=1, source_target_pairs={{0,4},{4,0},{8,12},{12,8},{16,20},{20,16},{24,28},{28,24},{1,5},{5... | collective-permute-start | bytes 786440 | tf_op jit(solution)/shard_map/ppermute | solution.py:181
  31.2 0.6 %collective-permute-done.6 = f32[32,2048]{1,0:T(8,128)S(1)} collective-permute-done((f32[32,2048]{1,0:T(8,128)S(1)}, f32[32,2048]{1,0:T(8,128)S(1)}, u32[]{:S(2)}, u32[]{:S(2)}) %collective-permute-start.6) | collective-permute-done | bytes 262176 | tf_op jit(solution)/shard_map/ppermute | solution.py:181
  31.8 1.6 %collective-permute-start.7 = (f32[16,2048]{1,0:T(8,128)S(1)}, f32[16,2048]{1,0:T(8,128)S(1)}, u32[]{:S(2)}, u32[]{:S(2)}) collective-permute-start(f32[16,2048]{1,0:T(8,128)S(1)} %slice.106), channel_id=1, source_target_pairs={{0,8},{4,12},{8,0},{12,4},{16,24},{20,28},{24,16},{28,20},{1,9},{5... | collective-permute-start | bytes 393224 | tf_op jit(solution)/shard_map/ppermute | solution.py:181
  33.4 0.6 %fusion = f32[512]{0:T(512)} fusion(f32[48,128]{1,0:T(8,128)S(1)} %pad_maximum_fusion.1, f32[64,128]{1,0:T(8,128)S(1)} %pad_maximum_fusion.message, s32[]{:T(128)S(6)} %select_n.3, f32[]{:T(128)} %bitcast.10), kind=kLoop, calls=%fused_computation.12 | loop fusion | flops 1536 | bytes 6152 | tf_op jit(solution)/shard_map/reshape | solution.py:240
  34.0 2.4 %collective-permute-done.3 = f32[32,2048]{1,0:T(8,128)S(1)} collective-permute-done((f32[32,2048]{1,0:T(8,128)S(1)}, f32[32,2048]{1,0:T(8,128)S(1)}, u32[]{:S(2)}, u32[]{:S(2)}) %collective-permute-start.3) | collective-permute-done | bytes 262176 | tf_op jit(solution)/shard_map/ppermute | solution.py:181
  36.5 1.6 %collective-permute-start.4 = (f32[16,2048]{1,0:T(8,128)S(1)}, f32[16,2048]{1,0:T(8,128)S(1)}, u32[]{:S(2)}, u32[]{:S(2)}) collective-permute-start(f32[16,2048]{1,0:T(8,128)S(1)} %slice.102), channel_id=1, source_target_pairs={{0,8},{4,12},{8,0},{12,4},{16,24},{20,28},{24,16},{28,20},{1,9},{5... | collective-permute-start | bytes 393224 | tf_op jit(solution)/shard_map/ppermute | solution.py:181
  38.2 2.8 %collective-permute-start.8 = (f32[8,2048]{1,0:T(8,128)S(1)}, f32[8,2048]{1,0:T(8,128)S(1)}, u32[]{:S(2)}, u32[]{:S(2)}) collective-permute-start(f32[8,2048]{1,0:T(8,128)S(1)} %slice.108), channel_id=1, source_target_pairs={{0,16},{4,20},{8,24},{12,28},{16,0},{20,4},{24,8},{28,12},{1,17},{... | collective-permute-start | bytes 196616 | tf_op jit(solution)/shard_map/ppermute | solution.py:181
  41.6 2.7 %collective-permute-start.5 = (f32[8,2048]{1,0:T(8,128)S(1)}, f32[8,2048]{1,0:T(8,128)S(1)}, u32[]{:S(2)}, u32[]{:S(2)}) collective-permute-start(f32[8,2048]{1,0:T(8,128)S(1)} %slice.104), channel_id=1, source_target_pairs={{0,16},{4,20},{8,24},{12,28},{16,0},{20,4},{24,8},{28,12},{1,17},{... | collective-permute-start | bytes 196616 | tf_op jit(solution)/shard_map/ppermute | solution.py:181
  44.3 2.5 %collective-permute-done.5 = f32[8,2048]{1,0:T(8,128)S(1)} collective-permute-done((f32[8,2048]{1,0:T(8,128)S(1)}, f32[8,2048]{1,0:T(8,128)S(1)}, u32[]{:S(2)}, u32[]{:S(2)}) %collective-permute-start.5) | collective-permute-done | bytes 65568 | tf_op jit(solution)/shard_map/ppermute | solution.py:181
  46.8 1.0 %arrange.1 = f32[4,64,128]{2,1,0:T(8,128)} custom-call(f32[8,2048]{1,0:T(8,128)S(1)} %slice_add_fusion.3.refs_0_, f32[8,2048]{1,0:T(8,128)S(1)} %slice_add_fusion.2.refs_1_), custom_call_target="tpu_custom_call" | custom-call | tf_op jit(solution)/shard_map/arrange/pallas_call | solution.py:282
  (39 shorter events, 0.9 us)
Async XLA Ops:
  3.1 6.0 %collective-permute-start = (f32[36,128]{1,0:T(8,128)}, f32[36,128]{1,0:T(8,128)S(1)}, u32[]{:S(2)}, u32[]{:S(2)}) collective-permute-start(f32[36,128]{1,0:T(8,128)} %group_sum.1), channel_id=1, source_target_pairs={{0,4},{4,0},{8,12},{12,8},{16,20},{20,16},{24,28},{28,24},{1,5},{5... | collective-permute-start | bytes 55304 | tf_op jit(solution)/shard_map/ppermute | solution.py:181
  6.8 2.4 %copy-start.4 = (f32[36,128]{1,0:T(8,128)S(1)}, f32[36,128]{1,0:T(8,128)}, u32[]{:S(2)}) copy-start(f32[36,128]{1,0:T(8,128)} %group_sum.1) | copy-start | bytes 55300
  8.5 2.3 %copy-start.3 = (s32[64,16384]{1,0:T(8,128)S(1)}, s32[64,16384]{1,0:T(8,128)}, u32[]{:S(2)}) copy-start(s32[64,16384]{1,0:T(8,128)} %param.11) | copy-start | bytes 12582916
  9.2 3.8 %collective-permute-start.1 = (f32[40,128]{1,0:T(8,128)S(1)}, f32[40,128]{1,0:T(8,128)S(1)}, u32[]{:S(2)}, u32[]{:S(2)}) collective-permute-start(f32[40,128]{1,0:T(8,128)S(1)} %pad_maximum_fusion.2), channel_id=1, source_target_pairs={{0,8},{4,12},{8,0},{12,4},{16,24},{20,28},{24,16},{28,20},{1,9},{5... | collective-permute-start | bytes 61448 | tf_op jit(solution)/shard_map/ppermute | solution.py:181
  11.0 4.7 %copy-start.5 = (bf16[16384]{0:T(1024)(128)(2,1)S(1)}, bf16[16384]{0:T(1024)(128)(2,1)}, u32[]{:S(2)}) copy-start(bf16[16384]{0:T(1024)(128)(2,1)} %param.8) | copy-start | bytes 98308
  11.0 6.9 %copy-start = (f32[16384]{0:T(1024)S(1)}, f32[16384]{0:T(1024)}, u32[]{:S(2)}) copy-start(f32[16384]{0:T(1024)} %param.7) | copy-start | bytes 196612
  11.0 6.9 %copy-start.1 = (s32[16384]{0:T(1024)S(1)}, s32[16384]{0:T(1024)}, u32[]{:S(2)}) copy-start(s32[16384]{0:T(1024)} %param.9) | copy-start | bytes 196612
  11.0 6.9 %copy-start.2 = (s32[16384]{0:T(1024)S(1)}, s32[16384]{0:T(1024)}, u32[]{:S(2)}) copy-start(s32[16384]{0:T(1024)} %param.10) | copy-start | bytes 196612
  13.1 4.8 %collective-permute-start.2 = (f32[48,128]{1,0:T(8,128)S(1)}, f32[48,128]{1,0:T(8,128)S(1)}, u32[]{:S(2)}, u32[]{:S(2)}) collective-permute-start(f32[48,128]{1,0:T(8,128)S(1)} %pad_maximum_fusion.1), channel_id=1, source_target_pairs={{0,16},{4,20},{8,24},{12,28},{16,0},{20,4},{24,8},{28,12},{1,17},{... | collective-permute-start | bytes 73736 | tf_op jit(solution)/shard_map/ppermute | solution.py:181
  24.1 7.7 %collective-permute-start.6 = (f32[32,2048]{1,0:T(8,128)S(1)}, f32[32,2048]{1,0:T(8,128)S(1)}, u32[]{:S(2)}, u32[]{:S(2)}) collective-permute-start(f32[32,2048]{1,0:T(8,128)S(1)} %get-tuple-element.25), channel_id=1, source_target_pairs={{0,4},{4,0},{8,12},{12,8},{16,20},{20,16},{24,28},{28,24},{1,5},{5... | collective-permute-start | bytes 786440 | tf_op jit(solution)/shard_map/ppermute | solution.py:181
  30.0 6.4 %collective-permute-start.3 = (f32[32,2048]{1,0:T(8,128)S(1)}, f32[32,2048]{1,0:T(8,128)S(1)}, u32[]{:S(2)}, u32[]{:S(2)}) collective-permute-start(f32[32,2048]{1,0:T(8,128)S(1)} %get-tuple-element.22), channel_id=1, source_target_pairs={{0,4},{4,0},{8,12},{12,8},{16,20},{20,16},{24,28},{28,24},{1,5},{5... | collective-permute-start | bytes 786440 | tf_op jit(solution)/shard_map/ppermute | solution.py:181
  31.8 6.3 %collective-permute-start.7 = (f32[16,2048]{1,0:T(8,128)S(1)}, f32[16,2048]{1,0:T(8,128)S(1)}, u32[]{:S(2)}, u32[]{:S(2)}) collective-permute-start(f32[16,2048]{1,0:T(8,128)S(1)} %slice.106), channel_id=1, source_target_pairs={{0,8},{4,12},{8,0},{12,4},{16,24},{20,28},{24,16},{28,20},{1,9},{5... | collective-permute-start | bytes 393224 | tf_op jit(solution)/shard_map/ppermute | solution.py:181
  36.5 5.0 %collective-permute-start.4 = (f32[16,2048]{1,0:T(8,128)S(1)}, f32[16,2048]{1,0:T(8,128)S(1)}, u32[]{:S(2)}, u32[]{:S(2)}) collective-permute-start(f32[16,2048]{1,0:T(8,128)S(1)} %slice.102), channel_id=1, source_target_pairs={{0,8},{4,12},{8,0},{12,4},{16,24},{20,28},{24,16},{28,20},{1,9},{5... | collective-permute-start | bytes 393224 | tf_op jit(solution)/shard_map/ppermute | solution.py:181
  38.2 6.1 %collective-permute-start.8 = (f32[8,2048]{1,0:T(8,128)S(1)}, f32[8,2048]{1,0:T(8,128)S(1)}, u32[]{:S(2)}, u32[]{:S(2)}) collective-permute-start(f32[8,2048]{1,0:T(8,128)S(1)} %slice.108), channel_id=1, source_target_pairs={{0,16},{4,20},{8,24},{12,28},{16,0},{20,4},{24,8},{28,12},{1,17},{... | collective-permute-start | bytes 196616 | tf_op jit(solution)/shard_map/ppermute | solution.py:181
  41.6 5.2 %collective-permute-start.5 = (f32[8,2048]{1,0:T(8,128)S(1)}, f32[8,2048]{1,0:T(8,128)S(1)}, u32[]{:S(2)}, u32[]{:S(2)}) collective-permute-start(f32[8,2048]{1,0:T(8,128)S(1)} %slice.104), channel_id=1, source_target_pairs={{0,16},{4,20},{8,24},{12,28},{16,0},{20,4},{24,8},{28,12},{1,17},{... | collective-permute-start | bytes 196616 | tf_op jit(solution)/shard_map/ppermute | solution.py:181

commit v3 on v2

--- a/solution.py
+++ b/solution.py
@@ -11,14 +11,10 @@
 BINS = 64
 LEAVES = 32
 LANES = 128
-TERMS = 6
-TGRANT = 48
-K1_STEP = 32
-GRANT = 60
-WEIGHT = 8
 CHUNKS = 2
+CROWDED = 16.0
 F8 = jnp.float8_e4m3fn
-STREAM = pltpu.CompilerParams(vmem_limit_bytes=int(GRANT * 2**20))
+STREAM = pltpu.CompilerParams(vmem_limit_bytes=60 * 2**20)
 PARAMS = pltpu.CompilerParams(vmem_limit_bytes=48 * 2**20)
 
 
@@ -26,42 +22,42 @@
     blocks = gradient.shape[0]
     own = sizes.shape[0]
     high_count = message.shape[0] - own
-    rest, parts = gradient[...], []
-    for n in range(TERMS):
-        part = rest.astype(F8).astype(jnp.float32)
-        rest = (rest - part) * 16.0
-        parts.append(part)
+    exact = gradient[...]
+    first = exact.astype(jnp.bfloat16).astype(jnp.float32)
+    rest = exact - first
+    second = rest.astype(jnp.bfloat16).astype(jnp.float32)
+    parts = (first, second, rest - second)
     ids = groups[...]
     high, low = lax.shift_right_logical(ids, 7), ids & (LANES - 1)
-    high_levels = lax.broadcasted_iota(jnp.int32, (high_count, LANES), 0).astype(jnp.int8)
-    low_levels = lax.broadcasted_iota(jnp.int32, (LANES, LANES), 0).astype(jnp.int8)
-    zero, one = jnp.zeros((), F8), jnp.ones((), F8)
+    high_levels = lax.broadcasted_iota(jnp.int32, (high_count, LANES), 0).astype(jnp.int16)
+    low_levels = lax.broadcasted_iota(jnp.int32, (LANES, LANES), 0).astype(jnp.int16)
+    zero, one = jnp.zeros((), jnp.bfloat16), jnp.ones((), jnp.bfloat16)
 
     def spread(values, j, rows, dtype):
         return jnp.broadcast_to(values[j : j + 1], (rows, LANES)).astype(dtype)
 
-    total = jnp.zeros((TERMS * high_count, LANES), jnp.float32)
-    step = min(K1_STEP, blocks)
+    total = jnp.zeros((3 * high_count, LANES), jnp.float32)
+    step = min(32, blocks)
     for start in range(0, blocks, step):
         left, right = [], []
         for j in range(start, start + step):
-            here = spread(high, j, high_count, jnp.int8) == high_levels
+            here = spread(high, j, high_count, jnp.int16) == high_levels
             left.append(
                 jnp.concatenate(
-                    [jnp.where(here, spread(part, j, high_count, F8), zero) for part in parts], 0
+                    [jnp.where(here, spread(part, j, high_count, jnp.bfloat16), zero) for part in parts],
+                    0,
                 )
             )
-            right.append(jnp.where(spread(low, j, LANES, jnp.int8) == low_levels, one, zero))
+            right.append(jnp.where(spread(low, j, LANES, jnp.int16) == low_levels, one, zero))
         total += lax.dot_general(
             jnp.concatenate(left, 1),
             jnp.concatenate(right, 1),
             (((1,), (1,)), ((), ())),
             preferred_element_type=jnp.float32,
         )
-    result = total[(TERMS - 1) * high_count :]
-    for n in reversed(range(TERMS - 1)):
-        result = result * 0.0625 + total[n * high_count : (n + 1) * high_count]
-    message[:high_count] = result
+    message[:high_count] = (
+        total[:high_count] + (total[high_count : 2 * high_count] + total[2 * high_count :])
+    )
     message[high_count:] = sizes[...].astype(jnp.float32)
 
 
@@ -108,7 +104,9 @@
         level = jnp.where(big, level * 2.0**-power, level)
         scale = jnp.where(big, scale * 2.0**-power, scale)
         back = jnp.where(big, back * 2.0**power, back)
-    unscale[...] = jnp.full(unscale.shape, back, jnp.float32)
+    limit = jnp.sum(curve) * (CROWDED / (LEAVES * BINS))
+    is_first = lax.broadcasted_iota(jnp.int32, unscale.shape, 0) == 0
+    unscale[...] = jnp.where(is_first, back, limit)
 
     scaled = adjusted * scale
     adjusted_high = scaled.astype(F8).astype(jnp.float32)
@@ -141,20 +139,59 @@
         left[:, j * LANES : (j + 1) * LANES] = jnp.concatenate(parts, 0)
 
 
-def histogram_kernel(level_step, turned, left, unscale, keep, send):
-    base = pl.program_id(0) * level_step
-    bins = turned[...]
-    hot = []
-    for q in range(level_step):
-        level = (base + q).astype(jnp.int8)
-        hot.append(jnp.where(bins == level, jnp.ones((), F8), jnp.zeros((), F8)))
-    both = jnp.dot(left[...], jnp.concatenate(hot, 1), preferred_element_type=jnp.float32)
-    half = both.shape[0] // 2
-    total = both[:half] + both[half:] * 0.0625
+def histogram_kernel(level_step, turned, left, unscale, keep, send, largest):
+    step, steps = pl.program_id(0), pl.num_programs(0)
+    half = left.shape[0] // 2
+    row_count = left.shape[1]
+    span = level_step * LANES
     is_gradient = lax.broadcasted_iota(jnp.int32, (half, 1), 0) % 2 == 0
-    total = total * jnp.where(is_gradient, unscale[0:1, 0:1], 1.0)
-    keep[...] = total[: half // 2]
-    send[...] = total[half // 2 :]
+    factor = jnp.where(is_gradient, unscale[0:1, 0:1], 1.0)
+
+    def hot(bins, first_level, dtype):
+        one, zero = jnp.ones((), dtype), jnp.zeros((), dtype)
+        return jnp.concatenate(
+            [jnp.where(bins == (first_level + q).astype(jnp.int8), one, zero) for q in range(level_step)], 1
+        )
+
+    def store(step, total):
+        where = pl.ds(pl.multiple_of(step * span, span), span)
+        keep[:, where] = total[: half // 2]
+        send[:, where] = total[half // 2 :]
+
+    both = jnp.dot(
+        left[...], hot(turned[...], step * level_step, F8), preferred_element_type=jnp.float32
+    )
+    total = (both[:half] + both[half:] * 0.0625) * factor
+    store(step, total)
+
+    curve = jnp.where(is_gradient, 0.0, total)
+    curve = functools.reduce(jnp.maximum, [curve[:, n : n + LANES] for n in range(0, span, LANES)])
+    largest[...] = jnp.where(step == 0, curve, jnp.maximum(largest[...], curve))
+
+    @pl.when(step == steps - 1)
+    def _():
+        crowded = jnp.max(largest[...]) > jnp.max(unscale[1:2])
+
+        @pl.when(crowded)
+        def _():
+            block = min(1024, row_count)
+
+            def levels(n, nothing):
+                def rows(m, total):
+                    where = pl.ds(pl.multiple_of(m * block, block), block)
+                    weights = left[:half, where].astype(jnp.float32)
+                    weights += left[half:, where].astype(jnp.float32) * 0.0625
+                    return total + jnp.dot(
+                        weights.astype(jnp.bfloat16),
+                        hot(turned[where], n * level_step, jnp.bfloat16),
+                        preferred_element_type=jnp.float32,
+                    )
+
+                total = jnp.zeros((half, span), jnp.float32)
+                store(n, lax.fori_loop(0, row_count // block, rows, total) * factor)
+                return nothing
+
+            lax.fori_loop(0, steps, levels, 0)
 
 
 def arrange_kernel(*refs):
@@ -220,7 +257,7 @@
             out_shape=jax.ShapeDtypeStruct((row_count, LANES), jnp.int8),
             in_specs=[vmem],
             out_specs=vmem,
-            compiler_params=pltpu.CompilerParams(vmem_limit_bytes=TGRANT * 2**20),
+            compiler_params=PARAMS,
             cost_estimate=pl.CostEstimate(flops=0, bytes_accessed=4 * bins.size, transcendentals=0),
             name="turn_bins",
         )(bins)
@@ -263,10 +300,11 @@
                 grid=(levels // level_step,),
                 out_shape=[jax.ShapeDtypeStruct((LEAVES, levels * LANES), jnp.float32)] * 2,
                 in_specs=[whole(part), whole(left), whole(unscale)],
-                out_specs=[pl.BlockSpec((LEAVES, level_step * LANES), lambda i: (0, i))] * 2,
+                out_specs=[pl.BlockSpec((LEAVES, levels * LANES), lambda i: (0, 0))] * 2,
+                scratch_shapes=[pltpu.VMEM((2 * LEAVES, LANES), jnp.float32)],
                 compiler_params=PARAMS,
                 cost_estimate=pl.CostEstimate(
-                    flops=WEIGHT * LEAVES * levels * LANES * row_count, bytes_accessed=0, transcendentals=0
+                    flops=8 * LEAVES * levels * LANES * row_count, bytes_accessed=0, transcendentals=0
                 ),
                 name="histogram",
             )(part, left, unscale)

time: 48 us -> 48.8 us (1.017)
  Pallas kernels: 15.8 us -> 16.5 us
where the time goes in v3:
time: 48.8 us; the launch traced here: 48.6 us
  starting transfers between devices  18.5 us (38%)
  Pallas kernels  16.5 us (34%)
  waiting for transfers between devices  8.67 us (18%)
  local copies, waits for them, and re-layouts  2.67 us (5%)
  between operations  1.49 us (3%)
  other arithmetic  0.73 us (1%)
    ppermute x9, starting transfers between devices, exchange(): return lax.ppermute(value, axis, [(i, i ^ bit) for i in range(count)])  18.5 us
    pallas_call x2, Pallas kernels, shards(): pl.pallas_call(functools.partial(histogram_kernel, level_step), grid=(lev...  10.2 us
    ppermute x9, waiting for transfers between devices, exchange(): return lax.ppermute(value, axis, [(i, i ^ bit) for i in range(count)])  8.67 us
    pallas_call x1, Pallas kernels, shards(): pl.pallas_call(group_sum_kernel, grid=(1,), out_shape=jax.ShapeDtypeStruc...  2.94 us
    slice x2, local copies, waits for them, and re-layouts, shards(): turned.append(turn(bins[n * width:(n + 1) * width]))  1.87 us
    pallas_call x1, Pallas kernels, shards(): pl.pallas_call(functools.partial(weigh_kernel, owner_order), out_shape=(j...  1.22 us
    pallas_call x2, Pallas kernels, turn(): pl.pallas_call(turn_kernel, out_shape=jax.ShapeDtypeStruct((row_count, LA...  1.21 us
  transfers between devices with their start and end apart: 9, of which 6 were waited for; matrix products, arithmetic and copies ran while one was open for 7% of the time, Pallas kernels for 13%

profile of v3, /device:TPU:0, one launch (start us, length us, event | category | flops | bytes accessed | tf_op | source)
XLA Modules:
  0.0 48.6 jit_solution(5457655001372318281)
XLA Ops:
  0.6 2.9 %group_sum.1 = f32[36,128]{1,0:T(8,128)} custom-call(f32[128,128]{1,0:T(8,128)} %bitcast.11, s32[128,128]{1,0:T(8,128)} %bitcast.13, s32[4,128]{1,0:T(4,128)} %bitcast.16), custom_call_target="tpu_custom_call" | custom-call | tf_op jit(solution)/shard_map/group_sum/pallas_call | solution.py:244
  3.6 3.0 %collective-permute-start = (f32[36,128]{1,0:T(8,128)}, f32[36,128]{1,0:T(8,128)S(1)}, u32[]{:S(2)}, u32[]{:S(2)}) collective-permute-start(f32[36,128]{1,0:T(8,128)} %group_sum.1), channel_id=1, source_target_pairs={{0,4},{4,0},{8,12},{12,8},{16,20},{20,16},{24,28},{28,24},{1,5},{5... | collective-permute-start | bytes 55304 | tf_op jit(solution)/shard_map/ppermute | solution.py:218
  6.5 0.7 %slice.95 = f32[4,128]{1,0:T(4,128)S(1)} slice(f32[36,128]{1,0:T(8,128)} %group_sum.1), slice={[32:36], [0:128]} | slice | bytes 4096 | tf_op jit(solution)/shard_map/slice | solution.py:271
  7.3 1.7 %slice.74.bins = s32[32,16384]{1,0:T(8,128)S(1)} slice(s32[64,16384]{1,0:T(8,128)} %param.11), slice={[0:32], [0:16384]} | slice | bytes 4194304 | tf_op jit(solution)/shard_map/slice | solution.py:269
  9.0 0.6 %turn_bins.2.turned = s8[16384,128]{1,0:T(32,128)(4,1)S(1)} custom-call(s32[32,16384]{1,0:T(8,128)S(1)} %slice.74.bins), custom_call_target="tpu_custom_call" | custom-call | bytes 2097152 | tf_op jit(solution)/shard_map/turn_bins/pallas_call | solution.py:255
  9.7 1.6 %collective-permute-start.1 = (f32[40,128]{1,0:T(8,128)S(1)}, f32[40,128]{1,0:T(8,128)S(1)}, u32[]{:S(2)}, u32[]{:S(2)}) collective-permute-start(f32[40,128]{1,0:T(8,128)S(1)} %pad_maximum_fusion.2), channel_id=1, source_target_pairs={{0,8},{4,12},{8,0},{12,4},{16,24},{20,28},{24,16},{28,20},{1,9},{5... | collective-permute-start | bytes 61448 | tf_op jit(solution)/shard_map/ppermute | solution.py:218
  11.5 0.6 %turn_bins.3.turned = s8[16384,128]{1,0:T(32,128)(4,1)S(1)} custom-call(s32[32,16384]{1,0:T(8,128)S(1)} %slice.79.bins), custom_call_target="tpu_custom_call" | custom-call | bytes 2097152 | tf_op jit(solution)/shard_map/turn_bins/pallas_call | solution.py:255
  12.1 1.4 %collective-permute-done.1 = f32[40,128]{1,0:T(8,128)S(1)} collective-permute-done((f32[40,128]{1,0:T(8,128)S(1)}, f32[40,128]{1,0:T(8,128)S(1)}, u32[]{:S(2)}, u32[]{:S(2)}) %collective-permute-start.1) | collective-permute-done | bytes 20512 | tf_op jit(solution)/shard_map/ppermute | solution.py:218
  13.5 2.7 %collective-permute-start.2 = (f32[48,128]{1,0:T(8,128)S(1)}, f32[48,128]{1,0:T(8,128)S(1)}, u32[]{:S(2)}, u32[]{:S(2)}) collective-permute-start(f32[48,128]{1,0:T(8,128)S(1)} %pad_maximum_fusion.1), channel_id=1, source_target_pairs={{0,16},{4,20},{8,24},{12,28},{16,0},{20,4},{24,8},{28,12},{1,17},{... | collective-permute-start | bytes 73736 | tf_op jit(solution)/shard_map/ppermute | solution.py:218
  16.9 1.5 %collective-permute-done.2 = f32[48,128]{1,0:T(8,128)S(1)} collective-permute-done((f32[48,128]{1,0:T(8,128)S(1)}, f32[48,128]{1,0:T(8,128)S(1)}, u32[]{:S(2)}, u32[]{:S(2)}) %collective-permute-start.2) | collective-permute-done | bytes 24608 | tf_op jit(solution)/shard_map/ppermute | solution.py:218
  18.4 1.2 %weigh_rows.1 = (f8e4m3fn[128,16384]{1,0:T(32,128)(4,1)S(1)}, f32[8,128]{1,0:T(8,128)S(1)}) custom-call(f32[64,128]{1,0:T(8,128)S(1)} %pad_maximum_fusion.message, f32[1]{0:T(128)} %copy.9.ratio, f32[128,128]{1,0:T(8,128)S(1)} %bitcast.12, f32[128,128]{1,0:T(8,128)S(1)} %bitcast_convert_fusion.hessian, s32[128,128]{1,0:T(8,128)S(1)} %bitcast.14, ...), custom_call_target="tpu_custom_call" | custom-call | tf_op jit(solution)/shard_map/weigh_rows/pallas_call | solution.py:282
  19.6 5.1 %histogram.3 = (f32[32,2048]{1,0:T(8,128)S(1)}, f32[32,2048]{1,0:T(8,128)S(1)}) custom-call(s8[16384,128]{1,0:T(32,128)(4,1)S(1)} %turn_bins.3.turned, f8e4m3fn[128,16384]{1,0:T(32,128)(4,1)S(1)} %get-tuple-element.19.left, f32[8,128]{1,0:T(8,128)S(1)} %get-tuple-element.20.unscale), custom_call_target="tpu_custom_call" | custom-call | flops 8589934592 | tf_op jit(solution)/shard_map/histogram/pallas_call | solution.py:298
  24.7 1.0 %collective-permute-start.6 = (f32[32,2048]{1,0:T(8,128)S(1)}, f32[32,2048]{1,0:T(8,128)S(1)}, u32[]{:S(2)}, u32[]{:S(2)}) collective-permute-start(f32[32,2048]{1,0:T(8,128)S(1)} %get-tuple-element.25), channel_id=1, source_target_pairs={{0,4},{4,0},{8,12},{12,8},{16,20},{20,16},{24,28},{28,24},{1,5},{5... | collective-permute-start | bytes 786440 | tf_op jit(solution)/shard_map/ppermute | solution.py:218
  25.7 5.1 %histogram.2 = (f32[32,2048]{1,0:T(8,128)S(1)}, f32[32,2048]{1,0:T(8,128)S(1)}) custom-call(s8[16384,128]{1,0:T(32,128)(4,1)S(1)} %turn_bins.2.turned, f8e4m3fn[128,16384]{1,0:T(32,128)(4,1)S(1)} %get-tuple-element.19.left, f32[8,128]{1,0:T(8,128)S(1)} %get-tuple-element.20.unscale), custom_call_target="tpu_custom_call" | custom-call | flops 8589934592 | tf_op jit(solution)/shard_map/histogram/pallas_call | solution.py:298
  30.8 1.2 %collective-permute-start.3 = (f32[32,2048]{1,0:T(8,128)S(1)}, f32[32,2048]{1,0:T(8,128)S(1)}, u32[]{:S(2)}, u32[]{:S(2)}) collective-permute-start(f32[32,2048]{1,0:T(8,128)S(1)} %get-tuple-element.22), channel_id=1, source_target_pairs={{0,4},{4,0},{8,12},{12,8},{16,20},{20,16},{24,28},{28,24},{1,5},{5... | collective-permute-start | bytes 786440 | tf_op jit(solution)/shard_map/ppermute | solution.py:218
  32.3 1.6 %collective-permute-start.7 = (f32[16,2048]{1,0:T(8,128)S(1)}, f32[16,2048]{1,0:T(8,128)S(1)}, u32[]{:S(2)}, u32[]{:S(2)}) collective-permute-start(f32[16,2048]{1,0:T(8,128)S(1)} %slice.106), channel_id=1, source_target_pairs={{0,8},{4,12},{8,0},{12,4},{16,24},{20,28},{24,16},{28,20},{1,9},{5... | collective-permute-start | bytes 393224 | tf_op jit(solution)/shard_map/ppermute | solution.py:218
  33.9 0.6 %fusion = f32[512]{0:T(512)} fusion(f32[48,128]{1,0:T(8,128)S(1)} %pad_maximum_fusion.1, f32[64,128]{1,0:T(8,128)S(1)} %pad_maximum_fusion.message, s32[]{:T(128)S(6)} %select_n.3, f32[]{:T(128)} %bitcast.10), kind=kLoop, calls=%fused_computation.12 | loop fusion | flops 1536 | bytes 6152 | tf_op jit(solution)/shard_map/reshape | solution.py:277
  34.5 2.7 %collective-permute-done.3 = f32[32,2048]{1,0:T(8,128)S(1)} collective-permute-done((f32[32,2048]{1,0:T(8,128)S(1)}, f32[32,2048]{1,0:T(8,128)S(1)}, u32[]{:S(2)}, u32[]{:S(2)}) %collective-permute-start.3) | collective-permute-done | bytes 262176 | tf_op jit(solution)/shard_map/ppermute | solution.py:218
  37.2 1.6 %collective-permute-start.4 = (f32[16,2048]{1,0:T(8,128)S(1)}, f32[16,2048]{1,0:T(8,128)S(1)}, u32[]{:S(2)}, u32[]{:S(2)}) collective-permute-start(f32[16,2048]{1,0:T(8,128)S(1)} %slice.102), channel_id=1, source_target_pairs={{0,8},{4,12},{8,0},{12,4},{16,24},{20,28},{24,16},{28,20},{1,9},{5... | collective-permute-start | bytes 393224 | tf_op jit(solution)/shard_map/ppermute | solution.py:218
  38.9 2.8 %collective-permute-start.8 = (f32[8,2048]{1,0:T(8,128)S(1)}, f32[8,2048]{1,0:T(8,128)S(1)}, u32[]{:S(2)}, u32[]{:S(2)}) collective-permute-start(f32[8,2048]{1,0:T(8,128)S(1)} %slice.108), channel_id=1, source_target_pairs={{0,16},{4,20},{8,24},{12,28},{16,0},{20,4},{24,8},{28,12},{1,17},{... | collective-permute-start | bytes 196616 | tf_op jit(solution)/shard_map/ppermute | solution.py:218
  41.7 0.6 %collective-permute-done.4 = f32[16,2048]{1,0:T(8,128)S(1)} collective-permute-done((f32[16,2048]{1,0:T(8,128)S(1)}, f32[16,2048]{1,0:T(8,128)S(1)}, u32[]{:S(2)}, u32[]{:S(2)}) %collective-permute-start.4) | collective-permute-done | bytes 131104 | tf_op jit(solution)/shard_map/ppermute | solution.py:218
  42.3 3.1 %collective-permute-start.5 = (f32[8,2048]{1,0:T(8,128)S(1)}, f32[8,2048]{1,0:T(8,128)S(1)}, u32[]{:S(2)}, u32[]{:S(2)}) collective-permute-start(f32[8,2048]{1,0:T(8,128)S(1)} %slice.104), channel_id=1, source_target_pairs={{0,16},{4,20},{8,24},{12,28},{16,0},{20,4},{24,8},{28,12},{1,17},{... | collective-permute-start | bytes 196616 | tf_op jit(solution)/shard_map/ppermute | solution.py:218
  45.4 2.2 %collective-permute-done.5 = f32[8,2048]{1,0:T(8,128)S(1)} collective-permute-done((f32[8,2048]{1,0:T(8,128)S(1)}, f32[8,2048]{1,0:T(8,128)S(1)}, u32[]{:S(2)}, u32[]{:S(2)}) %collective-permute-start.5) | collective-permute-done | bytes 65568 | tf_op jit(solution)/shard_map/ppermute | solution.py:218
  47.6 1.0 %arrange.1 = f32[4,64,128]{2,1,0:T(8,128)} custom-call(f32[8,2048]{1,0:T(8,128)S(1)} %slice_add_fusion.3.refs_0_, f32[8,2048]{1,0:T(8,128)S(1)} %slice_add_fusion.2.refs_1_), custom_call_target="tpu_custom_call" | custom-call | tf_op jit(solution)/shard_map/arrange/pallas_call | solution.py:320
  (39 shorter events, 0.7 us)
Async XLA Ops:
  3.6 6.0 %collective-permute-start = (f32[36,128]{1,0:T(8,128)}, f32[36,128]{1,0:T(8,128)S(1)}, u32[]{:S(2)}, u32[]{:S(2)}) collective-permute-start(f32[36,128]{1,0:T(8,128)} %group_sum.1), channel_id=1, source_target_pairs={{0,4},{4,0},{8,12},{12,8},{16,20},{20,16},{24,28},{28,24},{1,5},{5... | collective-permute-start | bytes 55304 | tf_op jit(solution)/shard_map/ppermute | solution.py:218
  7.3 2.4 %copy-start.4 = (f32[36,128]{1,0:T(8,128)S(1)}, f32[36,128]{1,0:T(8,128)}, u32[]{:S(2)}) copy-start(f32[36,128]{1,0:T(8,128)} %group_sum.1) | copy-start | bytes 55300
  9.0 2.3 %copy-start.3 = (s32[64,16384]{1,0:T(8,128)S(1)}, s32[64,16384]{1,0:T(8,128)}, u32[]{:S(2)}) copy-start(s32[64,16384]{1,0:T(8,128)} %param.11) | copy-start | bytes 12582916
  9.7 3.8 %collective-permute-start.1 = (f32[40,128]{1,0:T(8,128)S(1)}, f32[40,128]{1,0:T(8,128)S(1)}, u32[]{:S(2)}, u32[]{:S(2)}) collective-permute-start(f32[40,128]{1,0:T(8,128)S(1)} %pad_maximum_fusion.2), channel_id=1, source_target_pairs={{0,8},{4,12},{8,0},{12,4},{16,24},{20,28},{24,16},{28,20},{1,9},{5... | collective-permute-start | bytes 61448 | tf_op jit(solution)/shard_map/ppermute | solution.py:218
  11.5 4.7 %copy-start.5 = (bf16[16384]{0:T(1024)(128)(2,1)S(1)}, bf16[16384]{0:T(1024)(128)(2,1)}, u32[]{:S(2)}) copy-start(bf16[16384]{0:T(1024)(128)(2,1)} %param.8) | copy-start | bytes 98308
  11.5 6.9 %copy-start = (f32[16384]{0:T(1024)S(1)}, f32[16384]{0:T(1024)}, u32[]{:S(2)}) copy-start(f32[16384]{0:T(1024)} %param.7) | copy-start | bytes 196612
  11.5 6.9 %copy-start.1 = (s32[16384]{0:T(1024)S(1)}, s32[16384]{0:T(1024)}, u32[]{:S(2)}) copy-start(s32[16384]{0:T(1024)} %param.9) | copy-start | bytes 196612
  11.5 6.9 %copy-start.2 = (s32[16384]{0:T(1024)S(1)}, s32[16384]{0:T(1024)}, u32[]{:S(2)}) copy-start(s32[16384]{0:T(1024)} %param.10) | copy-start | bytes 196612
  13.5 4.8 %collective-permute-start.2 = (f32[48,128]{1,0:T(8,128)S(1)}, f32[48,128]{1,0:T(8,128)S(1)}, u32[]{:S(2)}, u32[]{:S(2)}) collective-permute-start(f32[48,128]{1,0:T(8,128)S(1)} %pad_maximum_fusion.1), channel_id=1, source_target_pairs={{0,16},{4,20},{8,24},{12,28},{16,0},{20,4},{24,8},{28,12},{1,17},{... | collective-permute-start | bytes 73736 | tf_op jit(solution)/shard_map/ppermute | solution.py:218
  24.7 7.6 %collective-permute-start.6 = (f32[32,2048]{1,0:T(8,128)S(1)}, f32[32,2048]{1,0:T(8,128)S(1)}, u32[]{:S(2)}, u32[]{:S(2)}) collective-permute-start(f32[32,2048]{1,0:T(8,128)S(1)} %get-tuple-element.25), channel_id=1, source_target_pairs={{0,4},{4,0},{8,12},{12,8},{16,20},{20,16},{24,28},{28,24},{1,5},{5... | collective-permute-start | bytes 786440 | tf_op jit(solution)/shard_map/ppermute | solution.py:218
  30.8 6.4 %collective-permute-start.3 = (f32[32,2048]{1,0:T(8,128)S(1)}, f32[32,2048]{1,0:T(8,128)S(1)}, u32[]{:S(2)}, u32[]{:S(2)}) collective-permute-start(f32[32,2048]{1,0:T(8,128)S(1)} %get-tuple-element.22), channel_id=1, source_target_pairs={{0,4},{4,0},{8,12},{12,8},{16,20},{20,16},{24,28},{28,24},{1,5},{5... | collective-permute-start | bytes 786440 | tf_op jit(solution)/shard_map/ppermute | solution.py:218
  32.3 6.6 %collective-permute-start.7 = (f32[16,2048]{1,0:T(8,128)S(1)}, f32[16,2048]{1,0:T(8,128)S(1)}, u32[]{:S(2)}, u32[]{:S(2)}) collective-permute-start(f32[16,2048]{1,0:T(8,128)S(1)} %slice.106), channel_id=1, source_target_pairs={{0,8},{4,12},{8,0},{12,4},{16,24},{20,28},{24,16},{28,20},{1,9},{5... | collective-permute-start | bytes 393224 | tf_op jit(solution)/shard_map/ppermute | solution.py:218
  37.2 5.0 %collective-permute-start.4 = (f32[16,2048]{1,0:T(8,128)S(1)}, f32[16,2048]{1,0:T(8,128)S(1)}, u32[]{:S(2)}, u32[]{:S(2)}) collective-permute-start(f32[16,2048]{1,0:T(8,128)S(1)} %slice.102), channel_id=1, source_target_pairs={{0,8},{4,12},{8,0},{12,4},{16,24},{20,28},{24,16},{28,20},{1,9},{5... | collective-permute-start | bytes 393224 | tf_op jit(solution)/shard_map/ppermute | solution.py:218
  38.9 6.5 %collective-permute-start.8 = (f32[8,2048]{1,0:T(8,128)S(1)}, f32[8,2048]{1,0:T(8,128)S(1)}, u32[]{:S(2)}, u32[]{:S(2)}) collective-permute-start(f32[8,2048]{1,0:T(8,128)S(1)} %slice.108), channel_id=1, source_target_pairs={{0,16},{4,20},{8,24},{12,28},{16,0},{20,4},{24,8},{28,12},{1,17},{... | collective-permute-start | bytes 196616 | tf_op jit(solution)/shard_map/ppermute | solution.py:218
  42.3 5.3 %collective-permute-start.5 = (f32[8,2048]{1,0:T(8,128)S(1)}, f32[8,2048]{1,0:T(8,128)S(1)}, u32[]{:S(2)}, u32[]{:S(2)}) collective-permute-start(f32[8,2048]{1,0:T(8,128)S(1)} %slice.104), channel_id=1, source_target_pairs={{0,16},{4,20},{8,24},{12,28},{16,0},{20,4},{24,8},{28,12},{1,17},{... | collective-permute-start | bytes 196616 | tf_op jit(solution)/shard_map/ppermute | solution.py:218

commit v4 on v3

--- a/solution.py
+++ b/solution.py
@@ -170,7 +170,7 @@
 
     @pl.when(step == steps - 1)
     def _():
-        crowded = jnp.max(largest[...]) > jnp.max(unscale[1:2])
+        crowded = jnp.max(largest[...] - unscale[1:2]) > 0.0
 
         @pl.when(crowded)
         def _():
@@ -291,7 +291,7 @@
         name="weigh_rows",
     )(message, variance_ratio, gradient, curve, groups, leaf_ids)
 
-    level_step = math.gcd(levels, 4)
+    level_step = math.gcd(levels, 8)
     pieces = []
     for part in turned:
         pieces.append(

time: 48.8 us -> 48.2 us (0.988)
  starting transfers between devices: 18.5 us -> 17.9 us
  Pallas kernels: 16.5 us -> 15.9 us
  waiting for transfers between devices: 8.67 us -> 9.22 us
    ppermute x9, starting transfers between devices: 18.5 us -> 17.9 us  [exchange(): return lax.ppermute(value, axis, [(i, i ^ bit) for i in range(count)])]
    pallas_call x2, Pallas kernels: 10.2 us -> 9.61 us  [shards(): pl.pallas_call(functools.partial(histogram_kernel, level_step), grid=(lev...]
    ppermute x9, waiting for transfers between devices: 8.67 us -> 9.22 us  [exchange(): return lax.ppermute(value, axis, [(i, i ^ bit) for i in range(count)])]
  transfers between devices with their start and end apart: 9 -> 9, of which waited for: 6 -> 8; matrix products, arithmetic and copies ran while one was open for 7% -> 7% of each run, Pallas kernels for 13% -> 13%
where the time goes in v4:
time: 48.2 us; the launch traced here: 47.9 us
  starting transfers between devices  17.9 us (37%)
  Pallas kernels  15.9 us (33%)
  waiting for transfers between devices  9.22 us (19%)
  local copies, waits for them, and re-layouts  2.67 us (6%)
  between operations  1.49 us (3%)
  other arithmetic  0.73 us (2%)
    ppermute x9, starting transfers between devices, exchange(): return lax.ppermute(value, axis, [(i, i ^ bit) for i in range(count)])  17.9 us
    pallas_call x2, Pallas kernels, shards(): pl.pallas_call(functools.partial(histogram_kernel, level_step), grid=(lev...  9.61 us
    ppermute x9, waiting for transfers between devices, exchange(): return lax.ppermute(value, axis, [(i, i ^ bit) for i in range(count)])  9.22 us
    pallas_call x1, Pallas kernels, shards(): pl.pallas_call(group_sum_kernel, grid=(1,), out_shape=jax.ShapeDtypeStruc...  2.94 us
    slice x2, local copies, waits for them, and re-layouts, shards(): turned.append(turn(bins[n * width:(n + 1) * width]))  1.87 us
    pallas_call x1, Pallas kernels, shards(): pl.pallas_call(functools.partial(weigh_kernel, owner_order), out_shape=(j...  1.22 us
    pallas_call x2, Pallas kernels, turn(): pl.pallas_call(turn_kernel, out_shape=jax.ShapeDtypeStruct((row_count, LA...  1.21 us
  transfers between devices with their start and end apart: 9, of which 8 were waited for; matrix products, arithmetic and copies ran while one was open for 7% of the time, Pallas kernels for 13%

profile of v4, /device:TPU:0, one launch (start us, length us, event | category | flops | bytes accessed | tf_op | source)
XLA Modules:
  0.0 47.9 jit_solution(16287383256395115722)
XLA Ops:
  0.6 2.9 %group_sum.1 = f32[36,128]{1,0:T(8,128)} custom-call(f32[128,128]{1,0:T(8,128)} %bitcast.11, s32[128,128]{1,0:T(8,128)} %bitcast.13, s32[4,128]{1,0:T(4,128)} %bitcast.16), custom_call_target="tpu_custom_call" | custom-call | tf_op jit(solution)/shard_map/group_sum/pallas_call | solution.py:244
  3.6 3.0 %collective-permute-start = (f32[36,128]{1,0:T(8,128)}, f32[36,128]{1,0:T(8,128)S(1)}, u32[]{:S(2)}, u32[]{:S(2)}) collective-permute-start(f32[36,128]{1,0:T(8,128)} %group_sum.1), channel_id=1, source_target_pairs={{0,4},{4,0},{8,12},{12,8},{16,20},{20,16},{24,28},{28,24},{1,5},{5... | collective-permute-start | bytes 55304 | tf_op jit(solution)/shard_map/ppermute | solution.py:218
  6.5 0.7 %slice.95 = f32[4,128]{1,0:T(4,128)S(1)} slice(f32[36,128]{1,0:T(8,128)} %group_sum.1), slice={[32:36], [0:128]} | slice | bytes 4096 | tf_op jit(solution)/shard_map/slice | solution.py:271
  7.3 1.7 %slice.74.bins = s32[32,16384]{1,0:T(8,128)S(1)} slice(s32[64,16384]{1,0:T(8,128)} %param.11), slice={[0:32], [0:16384]} | slice | bytes 4194304 | tf_op jit(solution)/shard_map/slice | solution.py:269
  9.0 0.6 %turn_bins.2.turned = s8[16384,128]{1,0:T(32,128)(4,1)S(1)} custom-call(s32[32,16384]{1,0:T(8,128)S(1)} %slice.74.bins), custom_call_target="tpu_custom_call" | custom-call | bytes 2097152 | tf_op jit(solution)/shard_map/turn_bins/pallas_call | solution.py:255
  9.7 1.6 %collective-permute-start.1 = (f32[40,128]{1,0:T(8,128)S(1)}, f32[40,128]{1,0:T(8,128)S(1)}, u32[]{:S(2)}, u32[]{:S(2)}) collective-permute-start(f32[40,128]{1,0:T(8,128)S(1)} %pad_maximum_fusion.2), channel_id=1, source_target_pairs={{0,8},{4,12},{8,0},{12,4},{16,24},{20,28},{24,16},{28,20},{1,9},{5... | collective-permute-start | bytes 61448 | tf_op jit(solution)/shard_map/ppermute | solution.py:218
  11.5 0.6 %turn_bins.3.turned = s8[16384,128]{1,0:T(32,128)(4,1)S(1)} custom-call(s32[32,16384]{1,0:T(8,128)S(1)} %slice.79.bins), custom_call_target="tpu_custom_call" | custom-call | bytes 2097152 | tf_op jit(solution)/shard_map/turn_bins/pallas_call | solution.py:255
  12.1 1.4 %collective-permute-done.1 = f32[40,128]{1,0:T(8,128)S(1)} collective-permute-done((f32[40,128]{1,0:T(8,128)S(1)}, f32[40,128]{1,0:T(8,128)S(1)}, u32[]{:S(2)}, u32[]{:S(2)}) %collective-permute-start.1) | collective-permute-done | bytes 20512 | tf_op jit(solution)/shard_map/ppermute | solution.py:218
  13.5 2.7 %collective-permute-start.2 = (f32[48,128]{1,0:T(8,128)S(1)}, f32[48,128]{1,0:T(8,128)S(1)}, u32[]{:S(2)}, u32[]{:S(2)}) collective-permute-start(f32[48,128]{1,0:T(8,128)S(1)} %pad_maximum_fusion.1), channel_id=1, source_target_pairs={{0,16},{4,20},{8,24},{12,28},{16,0},{20,4},{24,8},{28,12},{1,17},{... | collective-permute-start | bytes 73736 | tf_op jit(solution)/shard_map/ppermute | solution.py:218
  16.9 1.5 %collective-permute-done.2 = f32[48,128]{1,0:T(8,128)S(1)} collective-permute-done((f32[48,128]{1,0:T(8,128)S(1)}, f32[48,128]{1,0:T(8,128)S(1)}, u32[]{:S(2)}, u32[]{:S(2)}) %collective-permute-start.2) | collective-permute-done | bytes 24608 | tf_op jit(solution)/shard_map/ppermute | solution.py:218
  18.4 1.2 %weigh_rows.1 = (f8e4m3fn[128,16384]{1,0:T(32,128)(4,1)S(1)}, f32[8,128]{1,0:T(8,128)S(1)}) custom-call(f32[64,128]{1,0:T(8,128)S(1)} %pad_maximum_fusion.message, f32[1]{0:T(128)} %copy.9.ratio, f32[128,128]{1,0:T(8,128)S(1)} %bitcast.12, f32[128,128]{1,0:T(8,128)S(1)} %bitcast_convert_fusion.hessian, s32[128,128]{1,0:T(8,128)S(1)} %bitcast.14, ...), custom_call_target="tpu_custom_call" | custom-call | tf_op jit(solution)/shard_map/weigh_rows/pallas_call | solution.py:282
  19.6 4.8 %histogram.3 = (f32[32,2048]{1,0:T(8,128)S(1)}, f32[32,2048]{1,0:T(8,128)S(1)}) custom-call(s8[16384,128]{1,0:T(32,128)(4,1)S(1)} %turn_bins.3.turned, f8e4m3fn[128,16384]{1,0:T(32,128)(4,1)S(1)} %get-tuple-element.19.left, f32[8,128]{1,0:T(8,128)S(1)} %get-tuple-element.20.unscale), custom_call_target="tpu_custom_call" | custom-call | flops 8589934592 | tf_op jit(solution)/shard_map/histogram/pallas_call | solution.py:298
  24.4 1.0 %collective-permute-start.6 = (f32[32,2048]{1,0:T(8,128)S(1)}, f32[32,2048]{1,0:T(8,128)S(1)}, u32[]{:S(2)}, u32[]{:S(2)}) collective-permute-start(f32[32,2048]{1,0:T(8,128)S(1)} %get-tuple-element.25), channel_id=1, source_target_pairs={{0,4},{4,0},{8,12},{12,8},{16,20},{20,16},{24,28},{28,24},{1,5},{5... | collective-permute-start | bytes 786440 | tf_op jit(solution)/shard_map/ppermute | solution.py:218
  25.4 4.8 %histogram.2 = (f32[32,2048]{1,0:T(8,128)S(1)}, f32[32,2048]{1,0:T(8,128)S(1)}) custom-call(s8[16384,128]{1,0:T(32,128)(4,1)S(1)} %turn_bins.2.turned, f8e4m3fn[128,16384]{1,0:T(32,128)(4,1)S(1)} %get-tuple-element.19.left, f32[8,128]{1,0:T(8,128)S(1)} %get-tuple-element.20.unscale), custom_call_target="tpu_custom_call" | custom-call | flops 8589934592 | tf_op jit(solution)/shard_map/histogram/pallas_call | solution.py:298
  30.2 1.2 %collective-permute-start.3 = (f32[32,2048]{1,0:T(8,128)S(1)}, f32[32,2048]{1,0:T(8,128)S(1)}, u32[]{:S(2)}, u32[]{:S(2)}) collective-permute-start(f32[32,2048]{1,0:T(8,128)S(1)} %get-tuple-element.22), channel_id=1, source_target_pairs={{0,4},{4,0},{8,12},{12,8},{16,20},{20,16},{24,28},{28,24},{1,5},{5... | collective-permute-start | bytes 786440 | tf_op jit(solution)/shard_map/ppermute | solution.py:218
  31.4 0.9 %collective-permute-done.6 = f32[32,2048]{1,0:T(8,128)S(1)} collective-permute-done((f32[32,2048]{1,0:T(8,128)S(1)}, f32[32,2048]{1,0:T(8,128)S(1)}, u32[]{:S(2)}, u32[]{:S(2)}) %collective-permute-start.6) | collective-permute-done | bytes 262176 | tf_op jit(solution)/shard_map/ppermute | solution.py:218
  32.3 1.6 %collective-permute-start.7 = (f32[16,2048]{1,0:T(8,128)S(1)}, f32[16,2048]{1,0:T(8,128)S(1)}, u32[]{:S(2)}, u32[]{:S(2)}) collective-permute-start(f32[16,2048]{1,0:T(8,128)S(1)} %slice.106), channel_id=1, source_target_pairs={{0,8},{4,12},{8,0},{12,4},{16,24},{20,28},{24,16},{28,20},{1,9},{5... | collective-permute-start | bytes 393224 | tf_op jit(solution)/shard_map/ppermute | solution.py:218
  34.5 2.1 %collective-permute-done.3 = f32[32,2048]{1,0:T(8,128)S(1)} collective-permute-done((f32[32,2048]{1,0:T(8,128)S(1)}, f32[32,2048]{1,0:T(8,128)S(1)}, u32[]{:S(2)}, u32[]{:S(2)}) %collective-permute-start.3) | collective-permute-done | bytes 262176 | tf_op jit(solution)/shard_map/ppermute | solution.py:218
  36.7 1.6 %collective-permute-start.4 = (f32[16,2048]{1,0:T(8,128)S(1)}, f32[16,2048]{1,0:T(8,128)S(1)}, u32[]{:S(2)}, u32[]{:S(2)}) collective-permute-start(f32[16,2048]{1,0:T(8,128)S(1)} %slice.102), channel_id=1, source_target_pairs={{0,8},{4,12},{8,0},{12,4},{16,24},{20,28},{24,16},{28,20},{1,9},{5... | collective-permute-start | bytes 393224 | tf_op jit(solution)/shard_map/ppermute | solution.py:218
  38.6 2.6 %collective-permute-start.8 = (f32[8,2048]{1,0:T(8,128)S(1)}, f32[8,2048]{1,0:T(8,128)S(1)}, u32[]{:S(2)}, u32[]{:S(2)}) collective-permute-start(f32[8,2048]{1,0:T(8,128)S(1)} %slice.108), channel_id=1, source_target_pairs={{0,16},{4,20},{8,24},{12,28},{16,0},{20,4},{24,8},{28,12},{1,17},{... | collective-permute-start | bytes 196616 | tf_op jit(solution)/shard_map/ppermute | solution.py:218
  41.7 2.7 %collective-permute-start.5 = (f32[8,2048]{1,0:T(8,128)S(1)}, f32[8,2048]{1,0:T(8,128)S(1)}, u32[]{:S(2)}, u32[]{:S(2)}) collective-permute-start(f32[8,2048]{1,0:T(8,128)S(1)} %slice.104), channel_id=1, source_target_pairs={{0,16},{4,20},{8,24},{12,28},{16,0},{20,4},{24,8},{28,12},{1,17},{... | collective-permute-start | bytes 196616 | tf_op jit(solution)/shard_map/ppermute | solution.py:218
  44.4 1.3 %collective-permute-done.8 = f32[8,2048]{1,0:T(8,128)S(1)} collective-permute-done((f32[8,2048]{1,0:T(8,128)S(1)}, f32[8,2048]{1,0:T(8,128)S(1)}, u32[]{:S(2)}, u32[]{:S(2)}) %collective-permute-start.8) | collective-permute-done | bytes 65568 | tf_op jit(solution)/shard_map/ppermute | solution.py:218
  45.7 1.3 %collective-permute-done.5 = f32[8,2048]{1,0:T(8,128)S(1)} collective-permute-done((f32[8,2048]{1,0:T(8,128)S(1)}, f32[8,2048]{1,0:T(8,128)S(1)}, u32[]{:S(2)}, u32[]{:S(2)}) %collective-permute-start.5) | collective-permute-done | bytes 65568 | tf_op jit(solution)/shard_map/ppermute | solution.py:218
  47.0 1.0 %arrange.1 = f32[4,64,128]{2,1,0:T(8,128)} custom-call(f32[8,2048]{1,0:T(8,128)S(1)} %slice_add_fusion.3.refs_0_, f32[8,2048]{1,0:T(8,128)S(1)} %slice_add_fusion.2.refs_1_), custom_call_target="tpu_custom_call" | custom-call | tf_op jit(solution)/shard_map/arrange/pallas_call | solution.py:320
  (39 shorter events, 1.7 us)
Async XLA Ops:
  3.6 6.0 %collective-permute-start = (f32[36,128]{1,0:T(8,128)}, f32[36,128]{1,0:T(8,128)S(1)}, u32[]{:S(2)}, u32[]{:S(2)}) collective-permute-start(f32[36,128]{1,0:T(8,128)} %group_sum.1), channel_id=1, source_target_pairs={{0,4},{4,0},{8,12},{12,8},{16,20},{20,16},{24,28},{28,24},{1,5},{5... | collective-permute-start | bytes 55304 | tf_op jit(solution)/shard_map/ppermute | solution.py:218
  7.3 2.4 %copy-start.4 = (f32[36,128]{1,0:T(8,128)S(1)}, f32[36,128]{1,0:T(8,128)}, u32[]{:S(2)}) copy-start(f32[36,128]{1,0:T(8,128)} %group_sum.1) | copy-start | bytes 55300
  9.0 2.3 %copy-start.3 = (s32[64,16384]{1,0:T(8,128)S(1)}, s32[64,16384]{1,0:T(8,128)}, u32[]{:S(2)}) copy-start(s32[64,16384]{1,0:T(8,128)} %param.11) | copy-start | bytes 12582916
  9.7 3.8 %collective-permute-start.1 = (f32[40,128]{1,0:T(8,128)S(1)}, f32[40,128]{1,0:T(8,128)S(1)}, u32[]{:S(2)}, u32[]{:S(2)}) collective-permute-start(f32[40,128]{1,0:T(8,128)S(1)} %pad_maximum_fusion.2), channel_id=1, source_target_pairs={{0,8},{4,12},{8,0},{12,4},{16,24},{20,28},{24,16},{28,20},{1,9},{5... | collective-permute-start | bytes 61448 | tf_op jit(solution)/shard_map/ppermute | solution.py:218
  11.5 4.7 %copy-start.5 = (bf16[16384]{0:T(1024)(128)(2,1)S(1)}, bf16[16384]{0:T(1024)(128)(2,1)}, u32[]{:S(2)}) copy-start(bf16[16384]{0:T(1024)(128)(2,1)} %param.8) | copy-start | bytes 98308
  11.5 6.9 %copy-start = (f32[16384]{0:T(1024)S(1)}, f32[16384]{0:T(1024)}, u32[]{:S(2)}) copy-start(f32[16384]{0:T(1024)} %param.7) | copy-start | bytes 196612
  11.5 6.9 %copy-start.1 = (s32[16384]{0:T(1024)S(1)}, s32[16384]{0:T(1024)}, u32[]{:S(2)}) copy-start(s32[16384]{0:T(1024)} %param.9) | copy-start | bytes 196612
  11.5 6.9 %copy-start.2 = (s32[16384]{0:T(1024)S(1)}, s32[16384]{0:T(1024)}, u32[]{:S(2)}) copy-start(s32[16384]{0:T(1024)} %param.10) | copy-start | bytes 196612
  13.5 4.8 %collective-permute-start.2 = (f32[48,128]{1,0:T(8,128)S(1)}, f32[48,128]{1,0:T(8,128)S(1)}, u32[]{:S(2)}, u32[]{:S(2)}) collective-permute-start(f32[48,128]{1,0:T(8,128)S(1)} %pad_maximum_fusion.1), channel_id=1, source_target_pairs={{0,16},{4,20},{8,24},{12,28},{16,0},{20,4},{24,8},{28,12},{1,17},{... | collective-permute-start | bytes 73736 | tf_op jit(solution)/shard_map/ppermute | solution.py:218
  24.4 7.9 %collective-permute-start.6 = (f32[32,2048]{1,0:T(8,128)S(1)}, f32[32,2048]{1,0:T(8,128)S(1)}, u32[]{:S(2)}, u32[]{:S(2)}) collective-permute-start(f32[32,2048]{1,0:T(8,128)S(1)} %get-tuple-element.25), channel_id=1, source_target_pairs={{0,4},{4,0},{8,12},{12,8},{16,20},{20,16},{24,28},{28,24},{1,5},{5... | collective-permute-start | bytes 786440 | tf_op jit(solution)/shard_map/ppermute | solution.py:218
  30.2 6.4 %collective-permute-start.3 = (f32[32,2048]{1,0:T(8,128)S(1)}, f32[32,2048]{1,0:T(8,128)S(1)}, u32[]{:S(2)}, u32[]{:S(2)}) collective-permute-start(f32[32,2048]{1,0:T(8,128)S(1)} %get-tuple-element.22), channel_id=1, source_target_pairs={{0,4},{4,0},{8,12},{12,8},{16,20},{20,16},{24,28},{28,24},{1,5},{5... | collective-permute-start | bytes 786440 | tf_op jit(solution)/shard_map/ppermute | solution.py:218
  32.3 6.2 %collective-permute-start.7 = (f32[16,2048]{1,0:T(8,128)S(1)}, f32[16,2048]{1,0:T(8,128)S(1)}, u32[]{:S(2)}, u32[]{:S(2)}) collective-permute-start(f32[16,2048]{1,0:T(8,128)S(1)} %slice.106), channel_id=1, source_target_pairs={{0,8},{4,12},{8,0},{12,4},{16,24},{20,28},{24,16},{28,20},{1,9},{5... | collective-permute-start | bytes 393224 | tf_op jit(solution)/shard_map/ppermute | solution.py:218
  36.7 5.0 %collective-permute-start.4 = (f32[16,2048]{1,0:T(8,128)S(1)}, f32[16,2048]{1,0:T(8,128)S(1)}, u32[]{:S(2)}, u32[]{:S(2)}) collective-permute-start(f32[16,2048]{1,0:T(8,128)S(1)} %slice.102), channel_id=1, source_target_pairs={{0,8},{4,12},{8,0},{12,4},{16,24},{20,28},{24,16},{28,20},{1,9},{5... | collective-permute-start | bytes 393224 | tf_op jit(solution)/shard_map/ppermute | solution.py:218
  38.6 7.1 %collective-permute-start.8 = (f32[8,2048]{1,0:T(8,128)S(1)}, f32[8,2048]{1,0:T(8,128)S(1)}, u32[]{:S(2)}, u32[]{:S(2)}) collective-permute-start(f32[8,2048]{1,0:T(8,128)S(1)} %slice.108), channel_id=1, source_target_pairs={{0,16},{4,20},{8,24},{12,28},{16,0},{20,4},{24,8},{28,12},{1,17},{... | collective-permute-start | bytes 196616 | tf_op jit(solution)/shard_map/ppermute | solution.py:218
  41.7 5.2 %collective-permute-start.5 = (f32[8,2048]{1,0:T(8,128)S(1)}, f32[8,2048]{1,0:T(8,128)S(1)}, u32[]{:S(2)}, u32[]{:S(2)}) collective-permute-start(f32[8,2048]{1,0:T(8,128)S(1)} %slice.104), channel_id=1, source_target_pairs={{0,16},{4,20},{8,24},{12,28},{16,0},{20,4},{24,8},{28,12},{1,17},{... | collective-permute-start | bytes 196616 | tf_op jit(solution)/shard_map/ppermute | solution.py:218

commit v5 on v4

--- a/solution.py
+++ b/solution.py
@@ -194,23 +194,21 @@
             lax.fori_loop(0, steps, levels, 0)
 
 
-def arrange_kernel(*refs):
-    *parts, histograms = refs
-    share, features, _ = histograms.shape
-    width = features // len(parts)
+def arrange_kernel(own, *refs):
+    histograms = refs[-1]
+    share, width, _ = histograms.shape
     copies = LANES // width
     levels = BINS // copies
-    for c, own in enumerate(parts):
-        for l in range(share):
-            rows = []
-            for channel in range(2):
-                r = 2 * l + channel
-                block = jnp.concatenate(
-                    [own[r : r + 1, kk * LANES : (kk + 1) * LANES] for kk in range(levels)], 0
-                )
-                for p in range(copies):
-                    rows.append(block if p == 0 else jnp.roll(block, -p * width, axis=1))
-            histograms[l, c * width : (c + 1) * width] = jnp.concatenate(rows, 0).T[:width]
+    for l in range(share):
+        rows = []
+        for channel in range(2):
+            r = 2 * l + channel
+            block = jnp.concatenate(
+                [own[r : r + 1, kk * LANES : (kk + 1) * LANES] for kk in range(levels)], 0
+            )
+            for p in range(copies):
+                rows.append(block if p == 0 else jnp.roll(block, -p * width, axis=1))
+        histograms[l] = jnp.concatenate(rows, 0).T[:width]
 
 
 def exchange(value, axis, bit):
@@ -291,7 +289,7 @@
         name="weigh_rows",
     )(message, variance_ratio, gradient, curve, groups, leaf_ids)
 
-    level_step = math.gcd(levels, 8)
+    level_step = math.gcd(levels, 16)
     pieces = []
     for part in turned:
         pieces.append(
@@ -317,14 +315,19 @@
             keep, send = total[:middle], total[middle:]
         done.append(total)
 
-    histograms = pl.pallas_call(
-        arrange_kernel,
-        out_shape=jax.ShapeDtypeStruct((share, features, 2 * BINS), jnp.float32),
-        in_specs=[vmem] * len(done),
-        out_specs=vmem,
-        compiler_params=PARAMS,
-        name="arrange",
-    )(*done)
+    histograms = None
+    for c, total in enumerate(done):
+        before = [] if histograms is None else [histograms]
+        histograms = pl.pallas_call(
+            arrange_kernel,
+            grid=(1,),
+            out_shape=jax.ShapeDtypeStruct((share, features, 2 * BINS), jnp.float32),
+            in_specs=[whole(total)] + [pl.BlockSpec(memory_space=pl.ANY)] * len(before),
+            out_specs=pl.BlockSpec((share, width, 2 * BINS), lambda i, c=c: (0, c, 0)),
+            input_output_aliases={1: 0} if before else {},
+            compiler_params=PARAMS,
+            name="arrange",
+        )(total, *before)
     return histograms, own_means
 
 

time: 48.2 us -> 48.2 us (level)
  starting transfers between devices: 17.9 us -> 17.1 us
  Pallas kernels: 15.9 us -> 16.5 us
    ppermute x9, starting transfers between devices: 17.9 us -> 17.1 us  [exchange(): return lax.ppermute(value, axis, [(i, i ^ bit) for i in range(count)])]
    pallas_call x1 -> x2, Pallas kernels: 0.96 us -> 1.66 us  [shards(): pl.pallas_call(arrange_kernel, grid=(1,), out_shape=jax.ShapeDtypeStruct(...]
  transfers between devices with their start and end apart: 9 -> 9, of which waited for: 8 -> 6; matrix products, arithmetic and copies ran while one was open for 7% -> 7% of each run, Pallas kernels for 13% -> 14%
where the time goes in v5:
time: 48.2 us; the launch traced here: 48 us
  starting transfers between devices  17.1 us (35%)
  Pallas kernels  16.5 us (34%)
  waiting for transfers between devices  9.52 us (20%)
  local copies, waits for them, and re-layouts  2.67 us (6%)
  between operations  1.49 us (3%)
  other arithmetic  0.73 us (2%)
    ppermute x9, starting transfers between devices, exchange(): return lax.ppermute(value, axis, [(i, i ^ bit) for i in range(count)])  17.1 us
    ppermute x9, waiting for transfers between devices, exchange(): return lax.ppermute(value, axis, [(i, i ^ bit) for i in range(count)])  9.52 us
    pallas_call x2, Pallas kernels, shards(): pl.pallas_call(functools.partial(histogram_kernel, level_step), grid=(lev...  9.43 us
    pallas_call x1, Pallas kernels, shards(): pl.pallas_call(group_sum_kernel, grid=(1,), out_shape=jax.ShapeDtypeStruc...  2.94 us
    slice x2, local copies, waits for them, and re-layouts, shards(): turned.append(turn(bins[n * width:(n + 1) * width]))  1.87 us
    pallas_call x2, Pallas kernels, shards(): pl.pallas_call(arrange_kernel, grid=(1,), out_shape=jax.ShapeDtypeStruct(...  1.66 us
    pallas_call x1, Pallas kernels, shards(): pl.pallas_call(functools.partial(weigh_kernel, owner_order), out_shape=(j...  1.22 us
    pallas_call x2, Pallas kernels, turn(): pl.pallas_call(turn_kernel, out_shape=jax.ShapeDtypeStruct((row_count, LA...  1.21 us
  transfers between devices with their start and end apart: 9, of which 6 were waited for; matrix products, arithmetic and copies ran while one was open for 7% of the time, Pallas kernels for 14%

profile of v5, /device:TPU:0, one launch (start us, length us, event | category | flops | bytes accessed | tf_op | source)
XLA Modules:
  0.0 48.0 jit_solution(1020611013417871263)
XLA Ops:
  0.6 2.9 %group_sum.1 = f32[36,128]{1,0:T(8,128)} custom-call(f32[128,128]{1,0:T(8,128)} %bitcast.11, s32[128,128]{1,0:T(8,128)} %bitcast.13, s32[4,128]{1,0:T(4,128)} %bitcast.16), custom_call_target="tpu_custom_call" | custom-call | tf_op jit(solution)/shard_map/group_sum/pallas_call | solution.py:242
  3.6 3.0 %collective-permute-start = (f32[36,128]{1,0:T(8,128)}, f32[36,128]{1,0:T(8,128)S(1)}, u32[]{:S(2)}, u32[]{:S(2)}) collective-permute-start(f32[36,128]{1,0:T(8,128)} %group_sum.1), channel_id=1, source_target_pairs={{0,4},{4,0},{8,12},{12,8},{16,20},{20,16},{24,28},{28,24},{1,5},{5... | collective-permute-start | bytes 55304 | tf_op jit(solution)/shard_map/ppermute | solution.py:216
  6.5 0.7 %slice.95 = f32[4,128]{1,0:T(4,128)S(1)} slice(f32[36,128]{1,0:T(8,128)} %group_sum.1), slice={[32:36], [0:128]} | slice | bytes 4096 | tf_op jit(solution)/shard_map/slice | solution.py:269
  7.3 1.7 %slice.74.bins = s32[32,16384]{1,0:T(8,128)S(1)} slice(s32[64,16384]{1,0:T(8,128)} %param.11), slice={[0:32], [0:16384]} | slice | bytes 4194304 | tf_op jit(solution)/shard_map/slice | solution.py:267
  9.0 0.6 %turn_bins.2.turned = s8[16384,128]{1,0:T(32,128)(4,1)S(1)} custom-call(s32[32,16384]{1,0:T(8,128)S(1)} %slice.74.bins), custom_call_target="tpu_custom_call" | custom-call | bytes 2097152 | tf_op jit(solution)/shard_map/turn_bins/pallas_call | solution.py:253
  9.7 1.6 %collective-permute-start.1 = (f32[40,128]{1,0:T(8,128)S(1)}, f32[40,128]{1,0:T(8,128)S(1)}, u32[]{:S(2)}, u32[]{:S(2)}) collective-permute-start(f32[40,128]{1,0:T(8,128)S(1)} %pad_maximum_fusion.2), channel_id=1, source_target_pairs={{0,8},{4,12},{8,0},{12,4},{16,24},{20,28},{24,16},{28,20},{1,9},{5... | collective-permute-start | bytes 61448 | tf_op jit(solution)/shard_map/ppermute | solution.py:216
  12.1 1.4 %collective-permute-done.1 = f32[40,128]{1,0:T(8,128)S(1)} collective-permute-done((f32[40,128]{1,0:T(8,128)S(1)}, f32[40,128]{1,0:T(8,128)S(1)}, u32[]{:S(2)}, u32[]{:S(2)}) %collective-permute-start.1) | collective-permute-done | bytes 20512 | tf_op jit(solution)/shard_map/ppermute | solution.py:216
  13.5 2.7 %collective-permute-start.2 = (f32[48,128]{1,0:T(8,128)S(1)}, f32[48,128]{1,0:T(8,128)S(1)}, u32[]{:S(2)}, u32[]{:S(2)}) collective-permute-start(f32[48,128]{1,0:T(8,128)S(1)} %pad_maximum_fusion.1), channel_id=1, source_target_pairs={{0,16},{4,20},{8,24},{12,28},{16,0},{20,4},{24,8},{28,12},{1,17},{... | collective-permute-start | bytes 73736 | tf_op jit(solution)/shard_map/ppermute | solution.py:216
  16.9 1.5 %collective-permute-done.2 = f32[48,128]{1,0:T(8,128)S(1)} collective-permute-done((f32[48,128]{1,0:T(8,128)S(1)}, f32[48,128]{1,0:T(8,128)S(1)}, u32[]{:S(2)}, u32[]{:S(2)}) %collective-permute-start.2) | collective-permute-done | bytes 24608 | tf_op jit(solution)/shard_map/ppermute | solution.py:216
  18.4 1.2 %weigh_rows.1 = (f8e4m3fn[128,16384]{1,0:T(32,128)(4,1)S(1)}, f32[8,128]{1,0:T(8,128)S(1)}) custom-call(f32[64,128]{1,0:T(8,128)S(1)} %pad_maximum_fusion.message, f32[1]{0:T(128)} %copy.11.ratio, f32[128,128]{1,0:T(8,128)S(1)} %bitcast.12, f32[128,128]{1,0:T(8,128)S(1)} %bitcast_convert_fusion.hessian, s32[128,128]{1,0:T(8,128)S(1)} %bitcast.14, ...), custom_call_target="tpu_custom_call" | custom-call | tf_op jit(solution)/shard_map/weigh_rows/pallas_call | solution.py:280
  19.6 4.8 %histogram.3 = (f32[32,2048]{1,0:T(8,128)S(1)}, f32[32,2048]{1,0:T(8,128)S(1)}) custom-call(s8[16384,128]{1,0:T(32,128)(4,1)S(1)} %turn_bins.2.turned, f8e4m3fn[128,16384]{1,0:T(32,128)(4,1)S(1)} %get-tuple-element.19.left, f32[8,128]{1,0:T(8,128)S(1)} %get-tuple-element.20.unscale), custom_call_target="tpu_custom_call" | custom-call | flops 8589934592 | tf_op jit(solution)/shard_map/histogram/pallas_call | solution.py:296
  24.4 1.0 %collective-permute-start.6 = (f32[32,2048]{1,0:T(8,128)S(1)}, f32[32,2048]{1,0:T(8,128)S(1)}, u32[]{:S(2)}, u32[]{:S(2)}) collective-permute-start(f32[32,2048]{1,0:T(8,128)S(1)} %get-tuple-element.25), channel_id=1, source_target_pairs={{0,4},{4,0},{8,12},{12,8},{16,20},{20,16},{24,28},{28,24},{1,5},{5... | collective-permute-start | bytes 786440 | tf_op jit(solution)/shard_map/ppermute | solution.py:216
  25.4 4.6 %histogram.2 = (f32[32,2048]{1,0:T(8,128)S(1)}, f32[32,2048]{1,0:T(8,128)S(1)}) custom-call(s8[16384,128]{1,0:T(32,128)(4,1)S(1)} %turn_bins.3.turned, f8e4m3fn[128,16384]{1,0:T(32,128)(4,1)S(1)} %get-tuple-element.19.left, f32[8,128]{1,0:T(8,128)S(1)} %get-tuple-element.20.unscale), custom_call_target="tpu_custom_call" | custom-call | flops 8589934592 | tf_op jit(solution)/shard_map/histogram/pallas_call | solution.py:296
  30.0 1.2 %collective-permute-start.3 = (f32[32,2048]{1,0:T(8,128)S(1)}, f32[32,2048]{1,0:T(8,128)S(1)}, u32[]{:S(2)}, u32[]{:S(2)}) collective-permute-start(f32[32,2048]{1,0:T(8,128)S(1)} %get-tuple-element.22), channel_id=1, source_target_pairs={{0,4},{4,0},{8,12},{12,8},{16,20},{20,16},{24,28},{28,24},{1,5},{5... | collective-permute-start | bytes 786440 | tf_op jit(solution)/shard_map/ppermute | solution.py:216
  31.2 1.3 %collective-permute-done.6 = f32[32,2048]{1,0:T(8,128)S(1)} collective-permute-done((f32[32,2048]{1,0:T(8,128)S(1)}, f32[32,2048]{1,0:T(8,128)S(1)}, u32[]{:S(2)}, u32[]{:S(2)}) %collective-permute-start.6) | collective-permute-done | bytes 262176 | tf_op jit(solution)/shard_map/ppermute | solution.py:216
  32.5 1.6 %collective-permute-start.7 = (f32[16,2048]{1,0:T(8,128)S(1)}, f32[16,2048]{1,0:T(8,128)S(1)}, u32[]{:S(2)}, u32[]{:S(2)}) collective-permute-start(f32[16,2048]{1,0:T(8,128)S(1)} %slice.106), channel_id=1, source_target_pairs={{0,8},{4,12},{8,0},{12,4},{16,24},{20,28},{24,16},{28,20},{1,9},{5... | collective-permute-start | bytes 393224 | tf_op jit(solution)/shard_map/ppermute | solution.py:216
  34.7 1.8 %collective-permute-done.3 = f32[32,2048]{1,0:T(8,128)S(1)} collective-permute-done((f32[32,2048]{1,0:T(8,128)S(1)}, f32[32,2048]{1,0:T(8,128)S(1)}, u32[]{:S(2)}, u32[]{:S(2)}) %collective-permute-start.3) | collective-permute-done | bytes 262176 | tf_op jit(solution)/shard_map/ppermute | solution.py:216
  36.5 1.6 %collective-permute-start.4 = (f32[16,2048]{1,0:T(8,128)S(1)}, f32[16,2048]{1,0:T(8,128)S(1)}, u32[]{:S(2)}, u32[]{:S(2)}) collective-permute-start(f32[16,2048]{1,0:T(8,128)S(1)} %slice.102), channel_id=1, source_target_pairs={{0,8},{4,12},{8,0},{12,4},{16,24},{20,28},{24,16},{28,20},{1,9},{5... | collective-permute-start | bytes 393224 | tf_op jit(solution)/shard_map/ppermute | solution.py:216
  38.1 1.5 %collective-permute-done.7 = f32[16,2048]{1,0:T(8,128)S(1)} collective-permute-done((f32[16,2048]{1,0:T(8,128)S(1)}, f32[16,2048]{1,0:T(8,128)S(1)}, u32[]{:S(2)}, u32[]{:S(2)}) %collective-permute-start.7) | collective-permute-done | bytes 131104 | tf_op jit(solution)/shard_map/ppermute | solution.py:216
  39.7 1.8 %collective-permute-start.8 = (f32[8,2048]{1,0:T(8,128)S(1)}, f32[8,2048]{1,0:T(8,128)S(1)}, u32[]{:S(2)}, u32[]{:S(2)}) collective-permute-start(f32[8,2048]{1,0:T(8,128)S(1)} %slice.108), channel_id=1, source_target_pairs={{0,16},{4,20},{8,24},{12,28},{16,0},{20,4},{24,8},{28,12},{1,17},{... | collective-permute-start | bytes 196616 | tf_op jit(solution)/shard_map/ppermute | solution.py:216
  41.6 2.7 %collective-permute-start.5 = (f32[8,2048]{1,0:T(8,128)S(1)}, f32[8,2048]{1,0:T(8,128)S(1)}, u32[]{:S(2)}, u32[]{:S(2)}) collective-permute-start(f32[8,2048]{1,0:T(8,128)S(1)} %slice.104), channel_id=1, source_target_pairs={{0,16},{4,20},{8,24},{12,28},{16,0},{20,4},{24,8},{28,12},{1,17},{... | collective-permute-start | bytes 196616 | tf_op jit(solution)/shard_map/ppermute | solution.py:216
  44.2 2.1 %collective-permute-done.8 = f32[8,2048]{1,0:T(8,128)S(1)} collective-permute-done((f32[8,2048]{1,0:T(8,128)S(1)}, f32[8,2048]{1,0:T(8,128)S(1)}, u32[]{:S(2)}, u32[]{:S(2)}) %collective-permute-start.8) | collective-permute-done | bytes 65568 | tf_op jit(solution)/shard_map/ppermute | solution.py:216
  46.3 0.8 %arrange.2.refs_0_ = f32[4,64,128]{2,1,0:T(8,128)} custom-call(f32[8,2048]{1,0:T(8,128)S(1)} %slice_add_fusion.2.own), custom_call_target="tpu_custom_call" | custom-call | tf_op jit(solution)/shard_map/arrange/pallas_call | solution.py:321
  47.2 0.8 %arrange.3 = f32[4,64,128]{2,1,0:T(8,128)} custom-call(f32[8,2048]{1,0:T(8,128)S(1)} %slice_add_fusion.3.own, f32[4,64,128]{2,1,0:T(8,128)} %arrange.2.refs_0_), custom_call_target="tpu_custom_call", output_to_operand_aliasing={{}: (1, {})} | custom-call | tf_op jit(solution)/shard_map/arrange/pallas_call | solution.py:321
  (40 shorter events, 1.6 us)
Async XLA Ops:
  3.6 6.0 %collective-permute-start = (f32[36,128]{1,0:T(8,128)}, f32[36,128]{1,0:T(8,128)S(1)}, u32[]{:S(2)}, u32[]{:S(2)}) collective-permute-start(f32[36,128]{1,0:T(8,128)} %group_sum.1), channel_id=1, source_target_pairs={{0,4},{4,0},{8,12},{12,8},{16,20},{20,16},{24,28},{28,24},{1,5},{5... | collective-permute-start | bytes 55304 | tf_op jit(solution)/shard_map/ppermute | solution.py:216
  7.3 2.4 %copy-start.4 = (f32[36,128]{1,0:T(8,128)S(1)}, f32[36,128]{1,0:T(8,128)}, u32[]{:S(2)}) copy-start(f32[36,128]{1,0:T(8,128)} %group_sum.1) | copy-start | bytes 55300
  9.0 2.3 %copy-start.3 = (s32[64,16384]{1,0:T(8,128)S(1)}, s32[64,16384]{1,0:T(8,128)}, u32[]{:S(2)}) copy-start(s32[64,16384]{1,0:T(8,128)} %param.11) | copy-start | bytes 12582916
  9.7 3.8 %collective-permute-start.1 = (f32[40,128]{1,0:T(8,128)S(1)}, f32[40,128]{1,0:T(8,128)S(1)}, u32[]{:S(2)}, u32[]{:S(2)}) collective-permute-start(f32[40,128]{1,0:T(8,128)S(1)} %pad_maximum_fusion.2), channel_id=1, source_target_pairs={{0,8},{4,12},{8,0},{12,4},{16,24},{20,28},{24,16},{28,20},{1,9},{5... | collective-permute-start | bytes 61448 | tf_op jit(solution)/shard_map/ppermute | solution.py:216
  11.4 4.7 %copy-start.5 = (bf16[16384]{0:T(1024)(128)(2,1)S(1)}, bf16[16384]{0:T(1024)(128)(2,1)}, u32[]{:S(2)}) copy-start(bf16[16384]{0:T(1024)(128)(2,1)} %param.8) | copy-start | bytes 98308
  11.5 6.9 %copy-start = (f32[16384]{0:T(1024)S(1)}, f32[16384]{0:T(1024)}, u32[]{:S(2)}) copy-start(f32[16384]{0:T(1024)} %param.7) | copy-start | bytes 196612
  11.5 6.9 %copy-start.1 = (s32[16384]{0:T(1024)S(1)}, s32[16384]{0:T(1024)}, u32[]{:S(2)}) copy-start(s32[16384]{0:T(1024)} %param.9) | copy-start | bytes 196612
  11.5 6.9 %copy-start.2 = (s32[16384]{0:T(1024)S(1)}, s32[16384]{0:T(1024)}, u32[]{:S(2)}) copy-start(s32[16384]{0:T(1024)} %param.10) | copy-start | bytes 196612
  13.5 4.8 %collective-permute-start.2 = (f32[48,128]{1,0:T(8,128)S(1)}, f32[48,128]{1,0:T(8,128)S(1)}, u32[]{:S(2)}, u32[]{:S(2)}) collective-permute-start(f32[48,128]{1,0:T(8,128)S(1)} %pad_maximum_fusion.1), channel_id=1, source_target_pairs={{0,16},{4,20},{8,24},{12,28},{16,0},{20,4},{24,8},{28,12},{1,17},{... | collective-permute-start | bytes 73736 | tf_op jit(solution)/shard_map/ppermute | solution.py:216
  24.4 8.1 %collective-permute-start.6 = (f32[32,2048]{1,0:T(8,128)S(1)}, f32[32,2048]{1,0:T(8,128)S(1)}, u32[]{:S(2)}, u32[]{:S(2)}) collective-permute-start(f32[32,2048]{1,0:T(8,128)S(1)} %get-tuple-element.25), channel_id=1, source_target_pairs={{0,4},{4,0},{8,12},{12,8},{16,20},{20,16},{24,28},{28,24},{1,5},{5... | collective-permute-start | bytes 786440 | tf_op jit(solution)/shard_map/ppermute | solution.py:216
  30.0 6.5 %collective-permute-start.3 = (f32[32,2048]{1,0:T(8,128)S(1)}, f32[32,2048]{1,0:T(8,128)S(1)}, u32[]{:S(2)}, u32[]{:S(2)}) collective-permute-start(f32[32,2048]{1,0:T(8,128)S(1)} %get-tuple-element.22), channel_id=1, source_target_pairs={{0,4},{4,0},{8,12},{12,8},{16,20},{20,16},{24,28},{28,24},{1,5},{5... | collective-permute-start | bytes 786440 | tf_op jit(solution)/shard_map/ppermute | solution.py:216
  32.5 7.1 %collective-permute-start.7 = (f32[16,2048]{1,0:T(8,128)S(1)}, f32[16,2048]{1,0:T(8,128)S(1)}, u32[]{:S(2)}, u32[]{:S(2)}) collective-permute-start(f32[16,2048]{1,0:T(8,128)S(1)} %slice.106), channel_id=1, source_target_pairs={{0,8},{4,12},{8,0},{12,4},{16,24},{20,28},{24,16},{28,20},{1,9},{5... | collective-permute-start | bytes 393224 | tf_op jit(solution)/shard_map/ppermute | solution.py:216
  36.5 5.0 %collective-permute-start.4 = (f32[16,2048]{1,0:T(8,128)S(1)}, f32[16,2048]{1,0:T(8,128)S(1)}, u32[]{:S(2)}, u32[]{:S(2)}) collective-permute-start(f32[16,2048]{1,0:T(8,128)S(1)} %slice.102), channel_id=1, source_target_pairs={{0,8},{4,12},{8,0},{12,4},{16,24},{20,28},{24,16},{28,20},{1,9},{5... | collective-permute-start | bytes 393224 | tf_op jit(solution)/shard_map/ppermute | solution.py:216
  39.7 6.6 %collective-permute-start.8 = (f32[8,2048]{1,0:T(8,128)S(1)}, f32[8,2048]{1,0:T(8,128)S(1)}, u32[]{:S(2)}, u32[]{:S(2)}) collective-permute-start(f32[8,2048]{1,0:T(8,128)S(1)} %slice.108), channel_id=1, source_target_pairs={{0,16},{4,20},{8,24},{12,28},{16,0},{20,4},{24,8},{28,12},{1,17},{... | collective-permute-start | bytes 196616 | tf_op jit(solution)/shard_map/ppermute | solution.py:216
  41.6 5.6 %collective-permute-start.5 = (f32[8,2048]{1,0:T(8,128)S(1)}, f32[8,2048]{1,0:T(8,128)S(1)}, u32[]{:S(2)}, u32[]{:S(2)}) collective-permute-start(f32[8,2048]{1,0:T(8,128)S(1)} %slice.104), channel_id=1, source_target_pairs={{0,16},{4,20},{8,24},{12,28},{16,0},{20,4},{24,8},{28,12},{1,17},{... | collective-permute-start | bytes 196616 | tf_op jit(solution)/shard_map/ppermute | solution.py:216
